TPU v7x, 1024 devices: a whole 8x8x8 slice. The times are simulated.
1024 devices in a mesh: row: 64 (over y, x), rep: 16 (over z, core).
Axes of the slice: x: 8, y: 8, z: 8, core: 2. Of those that a mesh axis runs over, the one named last changes fastest.
Arguments:
- features: bfloat16 [32768, 256], P('row'), may hold values from -6 to 6
- w_self: bfloat16 [256, 256], replicated, may hold values from -0.375 to 0.375
- w_neigh: bfloat16 [256, 256], replicated, may hold values from -0.375 to 0.375
- bias_vector: float32 [256], replicated, may hold values from -3 to 3
- cotangent: bfloat16 [32768, 256], P('row'), may hold values from -6 to 6
- adj_values: bfloat16 [64, 16, 64, 128, 128], P('row', 'rep'), may hold values from 0 to 1.25, as said below
- src_slots: int32 [64, 16, 64], P('row', 'rep'), may hold values from 0 to 15, as said below
- dst_slots: int32 [64, 16, 64], P('row', 'rep'), may hold values from 0 to 3
- slot_counts: int32 [64, 16], P('row', 'rep'), may hold values from 0 to 64, as said below
Outputs:
- activations: bfloat16 [32768, 256], P(('row', 'rep'))
- grad_features: bfloat16 [32768, 256], P(('row', 'rep'))
- grad_self: float32 [256, 256], replicated
- grad_neigh: float32 [256, 256], replicated
- grad_bias: float32 [256], replicated
Inputs may be any that keep to these rules, and one draw needn't show every extreme that they name: `adj_values`: A is symmetric: whenever source tile b appears in a live slot of destination tile a, destination tile b lists source tile a in a live slot with the transposed tile, and a tile whose destination and source coincide is symmetric. Entries are zero or between 0.125 and 1.25. `src_slots`: an entry q names tile q % 4 of row block c * 4 + q // 4, where c is the replica index. `slot_counts`: live slots come first; at most 16 live slots of a row block and replica name one source row block; no pair of destination and source tiles repeats among them; they are ordered by source block, then destination tile, then source tile.
All inputs are finite; a program needn't handle non-finite values.
Results may differ from a plain program's by a relative error of at most 0.015.
Values may be sent and summed in bfloat16 or wider, within the bound.
A program may use at most 32 MiB of HBM per device.

v0:
```python
import math

import jax
import jax.numpy as jnp
from jax import lax
from jax.sharding import PartitionSpec as P


def spread(block, axis, holder):
    block = jnp.where(lax.axis_index(axis) == holder, block, jnp.zeros_like(block))
    return lax.psum(block, axis)


def neighbour_sum(field, tiles, sources, targets, live_count, sections):
    tile_size = tiles.shape[-1]
    block_rows, width = field.shape
    first_root = lax.axis_index("rep") * sections
    received = [spread(field, "row", first_root + section_no) for section_no in range(sections)]
    buffer = jnp.concatenate(received, 0).reshape(-1, tile_size, width)
    dest_count = block_rows // tile_size
    group_size = math.gcd(8, tiles.shape[0])
    dest_range = jnp.arange(dest_count, dtype=jnp.int32)
    group_range = jnp.arange(group_size, dtype=jnp.int32)

    def add_group(group_no, running):
        first_slot = group_no * group_size
        group_tiles = lax.dynamic_slice_in_dim(tiles, first_slot, group_size, 0)
        group_sources = lax.dynamic_slice_in_dim(sources, first_slot, group_size, 0)
        group_targets = lax.dynamic_slice_in_dim(targets, first_slot, group_size, 0)
        source_rows = jnp.take(buffer, group_sources, axis=0)
        products = jnp.einsum(
            "gab,gbf->gaf", group_tiles, source_rows, preferred_element_type=jnp.float32
        )
        alive = first_slot + group_range < live_count
        chosen = ((group_targets[:, None] == dest_range[None, :]) & alive[:, None]).astype(
            jnp.float32
        )
        return running + jnp.einsum("gt,gaf->taf", chosen, products)

    start_value = jnp.zeros((dest_count, tile_size, width), jnp.float32)
    summed = lax.fori_loop(0, (live_count + group_size - 1) // group_size, add_group, start_value)
    return summed.reshape(block_rows, width)


def shards(
    features, w_self, w_neigh, bias_vector, cotangent, adj_values, src_slots, dst_slots, slot_counts
):
    block_rows = features.shape[0]
    replicas = lax.axis_size("rep")
    sections = lax.axis_size("row") // replicas
    share_rows = block_rows // replicas
    offset = lax.axis_index("rep") * share_rows
    tiles = adj_values[0, 0]
    sources = src_slots[0, 0]
    targets = dst_slots[0, 0]
    live_count = slot_counts[0, 0]
    node_total = block_rows * lax.axis_size("row")
    slot_total = tiles.shape[0]
    dest_tiles = block_rows // tiles.shape[-1]
    norm_factor = 1.0 / math.sqrt(slot_total * replicas / dest_tiles)
    grad_factor = 1.0 / math.sqrt(node_total)
    partial_value = neighbour_sum(features, tiles, sources, targets, live_count, sections)
    aggregate_part = (
        lax.psum_scatter(partial_value, "rep", scatter_dimension=0, tiled=True) * norm_factor
    ).astype(jnp.bfloat16)
    aggregate = lax.all_gather(aggregate_part, "rep", axis=0, tiled=True)
    pre_act = (
        jnp.dot(features, w_self, preferred_element_type=jnp.float32)
        + jnp.dot(aggregate, w_neigh, preferred_element_type=jnp.float32)
        + bias_vector
    )
    activated = jax.nn.elu(pre_act).astype(jnp.bfloat16)
    grad_pre = (cotangent.astype(jnp.float32) * jnp.exp(jnp.minimum(pre_act, 0.0))).astype(
        jnp.bfloat16
    )
    message = jnp.einsum("nh,fh->nf", grad_pre, w_neigh, preferred_element_type=jnp.float32).astype(
        jnp.bfloat16
    )
    grad_share = lax.dynamic_slice_in_dim(grad_pre, offset, share_rows, 0)
    features_share = lax.dynamic_slice_in_dim(features, offset, share_rows, 0)
    activations = lax.dynamic_slice_in_dim(activated, offset, share_rows, 0)
    weight_terms = (
        jnp.einsum("nf,nh->fh", features_share, grad_share, preferred_element_type=jnp.float32),
        jnp.einsum("nf,nh->fh", aggregate_part, grad_share, preferred_element_type=jnp.float32),
        jnp.sum(grad_share.astype(jnp.float32), axis=0),
    )
    grad_self, grad_neigh, grad_bias = lax.psum(
        (weight_terms[0], weight_terms[1], weight_terms[2]), ("row", "rep")
    )
    back_partial = neighbour_sum(message, tiles, sources, targets, live_count, sections)
    returned = lax.psum_scatter(back_partial, "rep", scatter_dimension=0, tiled=True)
    self_term = jnp.einsum("nh,fh->nf", grad_share, w_self, preferred_element_type=jnp.float32)
    grad_features = (self_term + returned * norm_factor).astype(jnp.bfloat16)
    return (
        activations,
        grad_features,
        grad_self * grad_factor,
        grad_neigh * grad_factor,
        grad_bias * grad_factor,
    )


def solution(mesh):
    placed = (
        P("row", None),
        P(),
        P(),
        P(),
        P("row", None),
        P("row", "rep", None, None, None),
        P("row", "rep", None),
        P("row", "rep", None),
        P("row", "rep"),
    )
    return jax.shard_map(
        shards,
        mesh=mesh,
        in_specs=placed,
        out_specs=(P(("row", "rep"), None), P(("row", "rep"), None), P(), P(), P()),
        check_vma=False,
    )
```

profile of v0, /device:TPU:1, one launch (start us, length us, event | category | flops | bytes accessed | tf_op | source)
XLA Modules:
  0.0 827.8 jit_solution(1274887320370637397)
XLA Ops:
  7.2 1.9 broadcast_select_fusion.7
  9.9 181.6 %all-reduce.11.cloned.1.call-done = (bf16[512,256]{1,0:T(8,128)(2,1)}, bf16[512,256]{1,0:T(8,128)(2,1)}, bf16[512,256]{1,0:T(8,128)(2,1)}, bf16[512,256]{1,0:T(8,128)(2,1)}) async-done(((bf16[512,256]{1,0:T(8,128)(2,1)}, bf16[512,256]{1,0:T(8,128)(2,1)}, bf16[512,256]{1,0:T(8,128)(2,1)}, bf16[512,256]{1,0:T(8,128)(2,1)}), (bf16[512,256]{1,0:T(8,128)(2,1)}, bf16[512,256]{1,0:T(8,128)(2,1)}, ...) | async-done | bytes 1048592 | tf_op jit(solution)/shard_map/psum | solution.py:11
  191.5 1.3 pad_maximum_fusion
  192.9 27.7 %while.22 = (s32[]{:T(128)}, f32[4,128,256]{2,0,1:T(4,128)S(1)}, s32[]{:T(128)}, s32[64]{0:T(128)S(1)}, s32[]{:T(128)}, /*index=5*/bf16[64,128,128]{2,1,0:T(8,12...) while((s32[]{:T(128)}, f32[4,128,256]{2,0,1:T(4,128)S(1)}, ...), condition=%wide.region_5.7_spmd.clone, body=%wide.region_4.6_spmd.clone.sunk | while | flops 69600392 | bytes 3936703 | solution.py:41
  192.9 0.8 compare_and_fusion.4
  194.3 1.3 fusion.72
  195.7 0.7 convolution_add_fusion.6
  196.4 0.7 compare_and_fusion.4
  197.8 1.3 fusion.72
  199.2 0.7 convolution_add_fusion.6
  199.9 0.7 compare_and_fusion.4
  201.2 1.3 fusion.72
  202.6 0.7 convolution_add_fusion.6
  203.3 0.7 compare_and_fusion.4
  204.7 1.3 fusion.72
  206.1 0.7 convolution_add_fusion.6
  206.8 0.7 compare_and_fusion.4
  208.1 1.3 fusion.72
  209.5 0.7 convolution_add_fusion.6
  210.3 0.7 compare_and_fusion.4
  211.6 1.3 fusion.72
  213.0 0.7 convolution_add_fusion.6
  213.7 0.7 compare_and_fusion.4
  215.0 1.3 fusion.72
  216.4 0.7 convolution_add_fusion.6
  217.2 0.7 compare_and_fusion.4
  218.5 1.3 fusion.72
  219.9 0.7 convolution_add_fusion.6
  220.6 0.9 copy.14
  221.8 61.0 %reduce-scatter.3.cloned.1.call-done = f32[32,256]{1,0:T(8,128)} async-done(((f32[512,256]{1,0:T(8,128)}), f32[32,256]{1,0:T(8,128)}) %reduce-scatter.3.cloned.1.call-update) | async-done | bytes 32784 | tf_op jit(solution)/shard_map/reduce_scatter | solution.py:64
  282.8 0.8 multiply_convert_fusion.1
  283.6 18.0 %all_gather.3 = bf16[512,256]{1,0:T(8,128)(2,1)S(1)} all-gather(bf16[32,256]{1,0:T(8,128)(2,1)S(1)} %multiply_convert_fusion.1), channel_id=1, replica_groups=mesh['row'=64,'rep'=16] {'rep'}, dimensions={0}, use_global_device_ids=true | all-gather | bytes 278528 | tf_op jit(solution)/shard_map/all_gather | solution.py:66
  301.9 1.2 broadcast_select_fusion.6
  303.2 0.9 fusion.40
  304.1 0.9 fusion.42
  305.1 162.7 %all-reduce.9.cloned.1.call-done = (bf16[512,256]{1,0:T(8,128)(2,1)}, bf16[512,256]{1,0:T(8,128)(2,1)}, bf16[512,256]{1,0:T(8,128)(2,1)}, bf16[512,256]{1,0:T(8,128)(2,1)}) async-done(((bf16[512,256]{1,0:T(8,128)(2,1)}, bf16[512,256]{1,0:T(8,128)(2,1)}, bf16[512,256]{1,0:T(8,128)(2,1)}, bf16[512,256]{1,0:T(8,128)(2,1)}), (bf16[512,256]{1,0:T(8,128)(2,1)}, bf16[512,256]{1,0:T(8,128)(2,1)}, ...) | async-done | bytes 1048592 | tf_op jit(solution)/shard_map/psum | solution.py:11
  467.8 1.3 pad_maximum_fusion.1
  469.1 27.7 %while.23 = (s32[]{:T(128)}, f32[4,128,256]{2,0,1:T(4,128)S(1)}, s32[]{:T(128)}, s32[64]{0:T(128)S(1)}, s32[]{:T(128)}, /*index=5*/bf16[64,128,128]{2,1,0:T(8,12...) while((s32[]{:T(128)}, f32[4,128,256]{2,0,1:T(4,128)S(1)}, ...), condition=%wide.region_12.14_spmd.clone, body=%wide.region_11.13_spmd.clone.sunk | while | flops 69600392 | bytes 3936703 | solution.py:41
  469.2 0.7 compare_and_fusion.5
  470.5 1.3 fusion.77
  471.9 0.7 convolution_add_fusion.7
  472.6 0.7 compare_and_fusion.5
  473.9 1.3 fusion.77
  475.3 0.7 convolution_add_fusion.7
  476.1 0.7 compare_and_fusion.5
  477.4 1.3 fusion.77
  479.5 0.7 compare_and_fusion.5
  480.9 1.3 fusion.77
  482.3 0.7 convolution_add_fusion.7
  483.0 0.7 compare_and_fusion.5
  484.3 1.3 fusion.77
  486.4 0.7 compare_and_fusion.5
  487.8 1.3 fusion.77
  489.9 0.7 compare_and_fusion.5
  491.2 1.3 fusion.77
  493.4 0.7 compare_and_fusion.5
  494.7 1.3 fusion.77
  496.1 0.7 convolution_add_fusion.7
  496.8 0.9 copy.15
  497.8 117.2 %psum.87 = f32[256]{0:T(256)S(1)} all-reduce(f32[256]{0:T(256)S(1)} %convert_reduce_fusion), channel_id=1, replica_groups=mesh['row'=64,'rep'=16] {'row','rep'}, use_global_device_ids=true, to_apply=%region_17.19 | all-reduce | flops 256 | bytes 2048 | tf_op jit(solution)/shard_map/psum | solution.py:87
  616.1 146.7 %all-reduce.7.cloned.1.call-done = (f32[256,256]{1,0:T(8,128)}, f32[256,256]{1,0:T(8,128)}) async-done(((f32[256,256]{1,0:T(8,128)}, f32[256,256]{1,0:T(8,128)}), (f32[256,256]{1,0:T(8,128)}, f32[256,256]{1,0:T(8,128)})) %all-reduce.7.cloned.1.call-update) | async-done | bytes 524304 | tf_op jit(solution)/shard_map/psum | solution.py:87
  762.9 1.9 broadcast_multiply_fusion
  764.7 55.0 %reduce-scatter.5.cloned.1.call-done = f32[32,256]{1,0:T(8,128)} async-done(((f32[512,256]{1,0:T(8,128)}), f32[32,256]{1,0:T(8,128)}) %reduce-scatter.5.cloned.1.call-update) | async-done | bytes 32784 | tf_op jit(solution)/shard_map/reduce_scatter | solution.py:91
  819.7 1.5 fusion.37
  (83 shorter events, 15.7 us)
Async XLA Ops:
  7.2 294.4 %copy-start = (bf16[256,256]{1,0:T(8,128)(2,1)S(1)}, bf16[256,256]{1,0:T(8,128)(2,1)}, u32[]{:S(2)}) copy-start(bf16[256,256]{1,0:T(8,128)(2,1)} %param.17) | copy-start | bytes 393220
  7.2 184.4 %all-reduce.11.cloned.1.call-start = ((), (), s32[]{:S(2)}) async-start(), calls=%async_computation.6 | async-start | bytes 2097152 | tf_op jit(solution)/shard_map/psum | solution.py:11
  9.2 183.7 %copy-start.4 = (s32[1,1,64]{2,1,0:T(1,128)S(1)}, s32[1,1,64]{2,1,0:T(1,128)}, u32[]{:S(2)}) copy-start(s32[1,1,64]{2,1,0:T(1,128)} %param.21) | copy-start | bytes 772
  9.2 183.7 %copy-start.6 = (s32[1,1,64]{2,1,0:T(1,128)S(1)}, s32[1,1,64]{2,1,0:T(1,128)}, u32[]{:S(2)}) copy-start(s32[1,1,64]{2,1,0:T(1,128)} %param.22) | copy-start | bytes 772
  9.2 273.6 %reduce-scatter.3.cloned.1.call-start = ((), (), s32[]{:S(2)}) async-start(), calls=%async_computation.2 | async-start | bytes 557056 | tf_op jit(solution)/shard_map/reduce_scatter | solution.py:64
  192.9 28.7 %copy-start.1 = (bf16[512,256]{1,0:T(8,128)(2,1)S(1)}, bf16[512,256]{1,0:T(8,128)(2,1)}, u32[]{:S(2)}) copy-start(bf16[512,256]{1,0:T(8,128)(2,1)} %param.15) | copy-start | bytes 786436
  192.9 28.7 %copy-start.2 = (bf16[256,256]{1,0:T(8,128)(2,1)S(1)}, bf16[256,256]{1,0:T(8,128)(2,1)}, u32[]{:S(2)}) copy-start(bf16[256,256]{1,0:T(8,128)(2,1)} %param.16) | copy-start | bytes 393220
  220.6 80.9 %copy-start.3 = (bf16[512,256]{1,0:T(8,128)(2,1)S(1)}, bf16[512,256]{1,0:T(8,128)(2,1)}, u32[]{:S(2)}) copy-start(bf16[512,256]{1,0:T(8,128)(2,1)} %param.19) | copy-start | bytes 786436
  220.6 80.9 %copy-start.5 = (f32[256]{0:T(256)S(1)}, f32[256]{0:T(256)}, u32[]{:S(2)}) copy-start(f32[256]{0:T(256)} %param.18) | copy-start | bytes 3076
  221.5 246.3 %all-reduce.9.cloned.1.call-start = ((), (), s32[]{:S(2)}) async-start(), calls=%async_computation.5 | async-start | bytes 2097152 | tf_op jit(solution)/shard_map/psum | solution.py:11
  303.1 459.8 %all-reduce.7.cloned.1.call-start = ((), (), s32[]{:S(2)}) async-start(), calls=%async_computation.4 | async-start | bytes 1048576 | tf_op jit(solution)/shard_map/psum | solution.py:87
  305.0 514.7 %reduce-scatter.5.cloned.1.call-start = ((), (), s32[]{:S(2)}) async-start(), calls=%async_computation.3 | async-start | bytes 557056 | tf_op jit(solution)/shard_map/reduce_scatter | solution.py:91
Sparse Core Ops, SparseCore 0:
  12.0 179.5 all-reduce.10
  221.7 61.0 reduce-scatter.2
  303.2 164.5 all-reduce.8
  473.4 289.4 all-reduce.6
  766.1 53.6 reduce-scatter.4
where the time goes:
time: 831 us; the launch traced here: 828 us
  waiting for transfers between devices  607 us (73%)
  blocking collectives  135 us (16%)
  matrix products  37.6 us (5%)
  other arithmetic  20.1 us (2%)
  between operations  14.6 us (2%)
  local copies, waits for them, and re-layouts  12.5 us (2%)
    psum x2, waiting for transfers between devices, spread(): return lax.psum(block, axis)  344 us
    psum x1, waiting for transfers between devices, shards(): lax.psum((weight_terms[0], weight_terms[1], weight_terms[2]), ('row', 're...  147 us
    psum x1, blocking collectives, shards(): lax.psum((weight_terms[0], weight_terms[1], weight_terms[2]), ('row', 're...  117 us
    reduce_scatter x1, waiting for transfers between devices, shards(): lax.psum_scatter(partial_value, 'rep', scatter_dimension=0, tiled=True)  61 us
    reduce_scatter x1, waiting for transfers between devices, shards(): lax.psum_scatter(back_partial, 'rep', scatter_dimension=0, tiled=True)  55 us
    dot_general x16, matrix products, add_group(): jnp.einsum('gab,gbf->gaf', group_tiles, source_rows, preferred_element_ty...  21 us
    all_gather x1, blocking collectives, shards(): aggregate = lax.all_gather(aggregate_part, 'rep', axis=0, tiled=True)  18 us
  transfers between devices with their start and end apart: 5, of which 5 were waited for; matrix products, arithmetic and copies ran while one was open for 4% of the time, Pallas kernels for 0%

commit v1 on v0

v1 whole, which is shorter than its diff:
```python
import math

import jax
import jax.numpy as jnp
from jax import lax
from jax.experimental import pallas as pl
from jax.experimental.pallas import tpu as pltpu
from jax.sharding import PartitionSpec as P

RING = 8
HALF = 128
CHUNK = 32
TILE = 128
NB = 512
F = 256
MESH = pl.DeviceIdType.MESH
BF = jnp.bfloat16
F32 = jnp.float32


def wrap(value):
    return lax.rem(value, RING)


def dot_first(a, b):
    return lax.dot_general(a, b, (((0,), (0,)), ((), ())), preferred_element_type=F32)


def dot_last(a, b):
    return lax.dot_general(a, b, (((1,), (1,)), ((), ())), preferred_element_type=F32)


def kernel(
    norm_factor, grad_factor,
    feat, w_self, w_neigh, bias, cot, adj, src_slots, dst_slots, counts,
    act_out, gf_out, gs_out, gn_out, gb_out,
    tiles, dense, part, rec_a, rec_b, mid_a, mid_b, rec_a2, rec_b2, agg,
    f_rows, c_rows, g_own, a_own, act_ret, g_ret, gbuf, acc, back, rec_z, b_sib, b_own,
    gp, gp_rec, gx, gx_rec, gy, gz, gfull, gbias,
    tile_sem, s_t, r_t, s_adj, r_adj, s_a1, r_a1, s_b1, r_b1, s_a2, r_a2, s_b2, r_b2,
    s_agg, r_agg, s_ga1, r_ga1, s_gb1, r_gb1, s_ga2, r_ga2, s_gb2, r_gb2, s_ret, r_ret,
    s_gz, r_gz, s_gx, r_gx, s_gy, r_gy, s_hx, r_hx, s_hz, r_hz, s_hs, r_hs,
    s_z, r_z, s_sib, r_sib,
):
    row = lax.axis_index("row")
    rep = lax.axis_index("rep")
    y, x = row // RING, lax.rem(row, RING)
    z, k = rep // 2, lax.rem(rep, 2)
    sib = 1 - k

    def at(xx, yy, zz, kk):
        return (yy * RING + xx, zz * 2 + kk)

    def along(axis, d):
        if axis == "x":
            return at(wrap(x + d), y, z, k)
        if axis == "y":
            return at(x, wrap(y + d), z, k)
        return at(x, y, wrap(z + d), k)

    def remote(src, dst, send_sem, recv_sem, device):
        return pltpu.make_async_remote_copy(
            src_ref=src, dst_ref=dst, send_sem=send_sem, recv_sem=recv_sem,
            device_id=device, device_id_type=MESH,
        )

    def peers(fn, first=1):
        def step(d, carry):
            fn(d)
            return carry

        lax.fori_loop(first, RING, step, 0)

    own_chunk = rep
    worker_y = wrap(own_chunk)
    own_half = own_chunk // RING
    is_self = jnp.logical_and(worker_y == y, y == z)

    def worker(core):
        return at(x, worker_y, y, core)

    def owner(half):
        return at(x, z, 4 * half + y // 2, lax.rem(y, 2))

    def owner_is_self(half):
        return jnp.logical_and(is_self, own_half == half)

    barrier = pltpu.get_barrier_semaphore()

    def greet(device):
        pl.semaphore_signal(barrier, inc=1, device_id=device, device_id_type=MESH)

    def greet_peers(d):
        for core in (0, 1):
            greet(at(wrap(x + d), y, z, core))
            greet(at(x, wrap(y + d), z, core))
        greet(at(x, y, wrap(z + d), k))

    peers(greet_peers)
    greet(at(x, y, z, sib))
    for core in (0, 1):
        @pl.when(jnp.logical_not(jnp.logical_and(is_self, k == core)))
        def _():
            greet(worker(core))

        @pl.when(jnp.logical_not(owner_is_self(core)))
        def _():
            greet(owner(core))

    load = pltpu.make_async_copy(adj.at[0, 0], tiles, tile_sem)
    load.start()
    load.wait()
    live = counts[0, 0]

    def build(section, pointer):
        for t in range(4):
            for u in range(4):
                slot = jnp.minimum(pointer, 63)
                hit = jnp.logical_and(
                    pointer < live,
                    jnp.logical_and(
                        src_slots[0, 0, slot] == section * 4 + u, dst_slots[0, 0, slot] == t
                    ),
                )
                tile = tiles[slot]
                dense[4 * k + section, pl.ds(t * TILE, TILE), pl.ds(u * TILE, TILE)] = jnp.where(
                    hit, tile, jnp.zeros_like(tile)
                )
                pointer = pointer + hit.astype(jnp.int32)
        return pointer

    lax.fori_loop(0, 4, build, jnp.int32(0))

    def push(section, carry):
        product = dot_first(dense[4 * k + section], feat[...]).astype(BF)
        part[0, section] = product[:, :HALF]
        part[1, section] = product[:, HALF:]
        return carry

    lax.fori_loop(0, 4, push, 0)

    pl.semaphore_wait(barrier, 40 - 2 * is_self.astype(jnp.int32))

    mine_here = (x // 4) == k

    def a1_copy(section, lane):
        to_x = 4 * k + section
        d = wrap(to_x - x + RING)
        return remote(
            part.at[lane, section, pl.ds(0, 256)], rec_a.at[d],
            s_a1.at[section * 2 + lane], r_a1.at[d], at(to_x, y, z, lane),
        )

    def a1_start(section, carry):
        for lane in (0, 1):
            @pl.when(jnp.logical_not(jnp.logical_and(4 * k + section == x, k == lane)))
            def _():
                a1_copy(section, lane).start()
        return carry

    def b1_copy(d, lane):
        to_y = wrap(y + d)
        return remote(
            part.at[lane, :, pl.ds(256 + CHUNK * to_y, CHUNK)], rec_b.at[d, k],
            s_b1.at[d * 2 + lane], r_b1.at[d * 2 + k], at(x, to_y, z, lane),
        )

    def b1_start(d):
        for lane in (0, 1):
            b1_copy(d, lane).start()

    lax.fori_loop(0, 4, a1_start, 0)
    peers(b1_start)
    b1_copy_sib = remote(
        part.at[sib, :, pl.ds(256 + CHUNK * y, CHUNK)], rec_b.at[0, k],
        s_b1.at[0], r_b1.at[k], at(x, y, z, sib),
    )
    b1_copy_sib.start()
    rec_b[0, k] = part[k, :, pl.ds(pl.multiple_of(256 + CHUNK * y, CHUNK), CHUNK), :]

    @pl.when(mine_here)
    def _():
        rec_a[0] = part[k, x - 4 * k, pl.ds(0, 256), :]

    def t_copies(core):
        rows = pl.ds(CHUNK * own_chunk, CHUNK)
        return (
            remote(feat.at[rows], f_rows.at[own_half], s_t.at[core], r_t.at[own_half], worker(core)),
            remote(
                cot.at[rows, pl.ds(HALF * core, HALF)], c_rows.at[own_half],
                s_t.at[2 + core], r_t.at[2 + own_half], worker(core),
            ),
        )

    for core in (0, 1):
        @pl.when(jnp.logical_not(jnp.logical_and(is_self, k == core)))
        def _():
            for copy in t_copies(core):
                copy.start()

    @pl.when(is_self)
    def _():
        rows = pl.ds(pl.multiple_of(CHUNK * own_chunk, CHUNK), CHUNK)
        f_rows[own_half] = feat[rows, :]
        c_rows[own_half] = cot[rows, pl.ds(pl.multiple_of(HALF * k, HALF), HALF)]

    adj_copy = remote(
        dense.at[pl.ds(4 * k, 4)], dense.at[pl.ds(4 * k, 4)], s_adj.at[0], r_adj.at[0],
        at(x, y, z, sib),
    )
    adj_copy.start()

    for half in (0, 1):
        @pl.when(jnp.logical_not(owner_is_self(half)))
        def _():
            remote(f_rows.at[half], f_rows.at[half], s_t.at[0], r_t.at[half], owner(half)).wait_recv()
            remote(
                c_rows.at[half], c_rows.at[half], s_t.at[2], r_t.at[2 + half], owner(half)
            ).wait_recv()

    lanes = pl.ds(pl.multiple_of(HALF * k, HALF), HALF)
    rows64 = f_rows[...].reshape(64, F)
    self_part = jnp.dot(rows64, w_self[:, lanes], preferred_element_type=F32) + bias[:, lanes]

    def a1_wait(d):
        remote(rec_a.at[d], rec_a.at[d], s_a1.at[0], r_a1.at[d], at(x, y, z, sib)).wait_recv()

    @pl.when(jnp.logical_not(mine_here))
    def _():
        a1_wait(0)

    peers(a1_wait)

    def summed(ref):
        total = ref[0].astype(F32)
        for d in range(1, RING):
            total = total + ref[d].astype(F32)
        return total

    mid_a[...] = summed(rec_a).astype(BF).reshape(RING, CHUNK, HALF)

    def a2_copy(d):
        return remote(
            mid_a.at[wrap(y + d)], rec_a2.at[d], s_a2.at[d], r_a2.at[d], along("y", d)
        )

    peers(lambda d: a2_copy(d).start())
    rec_a2[0] = mid_a[y]

    def b1_wait(d):
        for core in (0, 1):
            remote(
                rec_b.at[d, core], rec_b.at[d, core], s_b1.at[0], r_b1.at[d * 2 + core],
                at(x, y, z, sib),
            ).wait_recv()

    remote(
        rec_b.at[0, sib], rec_b.at[0, sib], s_b1.at[0], r_b1.at[sib], at(x, y, z, sib)
    ).wait_recv()
    peers(b1_wait)
    mid_b[...] = summed(rec_b).astype(BF).reshape(RING, CHUNK, HALF)

    def b2_copy(d):
        return remote(
            mid_b.at[wrap(x + d)], rec_b2.at[d], s_b2.at[d], r_b2.at[d], along("x", d)
        )

    peers(lambda d: b2_copy(d).start())
    rec_b2[0] = mid_b[x]

    peers(lambda d: a2_copy(d).wait_recv())
    agg[k, pl.ds(0, CHUNK), :] = (summed(rec_a2) * norm_factor).astype(BF)
    peers(lambda d: b2_copy(d).wait_recv())
    agg[k, pl.ds(CHUNK, CHUNK), :] = (summed(rec_b2) * norm_factor).astype(BF)
    agg_copy = remote(agg.at[k], agg.at[k], s_agg.at[0], r_agg.at[0], at(x, y, z, sib))
    agg_copy.start()
    remote(agg.at[sib], agg.at[sib], s_agg.at[0], r_agg.at[0], at(x, y, z, sib)).wait_recv()

    pre = (
        self_part
        + jnp.dot(agg[0], w_neigh[pl.ds(0, HALF), lanes], preferred_element_type=F32)
        + jnp.dot(agg[1], w_neigh[pl.ds(HALF, HALF), lanes], preferred_element_type=F32)
    )
    low = jnp.exp(jnp.minimum(pre, 0.0))
    grad = (c_rows[...].reshape(64, HALF).astype(F32) * low).astype(BF)
    g_own[...] = grad.reshape(2, CHUNK, HALF)
    a_own[...] = jnp.where(pre > 0, pre, low - 1.0).astype(BF).reshape(
        2, CHUNK, HALF
    )

    place_a = gbuf.at[x, pl.ds(CHUNK * y, CHUNK)]
    place_b = gbuf.at[x, pl.ds(256 + CHUNK * y, CHUNK)]
    gbuf[x, pl.ds(pl.multiple_of(CHUNK * y, CHUNK), CHUNK), :] = g_own[0]
    gbuf[x, pl.ds(pl.multiple_of(256 + CHUNK * y, CHUNK), CHUNK), :] = g_own[1]

    def ga1_copy(d):
        return remote(g_own.at[0], place_a, s_ga1.at[d], r_ga1.at[d], along("y", d))

    def gb1_copy(d):
        return remote(g_own.at[1], place_b, s_gb1.at[d], r_gb1.at[d], along("x", d))

    def g1_start(d):
        ga1_copy(d).start()
        gb1_copy(d).start()

    peers(g1_start)

    def ret_copies(half):
        return (
            remote(a_own.at[half], act_ret.at[k], s_ret.at[half], r_ret.at[k], owner(half)),
            remote(g_own.at[half], g_ret.at[k], s_ret.at[2 + half], r_ret.at[2 + k], owner(half)),
        )

    for half in (0, 1):
        @pl.when(jnp.logical_not(owner_is_self(half)))
        def _():
            for copy in ret_copies(half):
                copy.start()

    @pl.when(is_self)
    def _():
        act_ret[k] = a_own[own_half]
        g_ret[k] = g_own[own_half]

    grad_s = dot_first(rows64, grad)
    grad_n = jnp.concatenate([dot_first(agg[0], grad), dot_first(agg[1], grad)], 0)
    terms = jnp.concatenate([grad_s, grad_n], 0).reshape(RING, 64, HALF)
    gp[:, pl.ds(0, 64), :] = terms
    col_sum = jnp.broadcast_to(jnp.sum(grad.astype(F32), axis=0, keepdims=True), (8, HALF))
    gp[:, pl.ds(64, 8), :] = jnp.broadcast_to(col_sum[None], (RING, 8, HALF))

    def gz_copy(d):
        return remote(gp.at[wrap(z + d)], gp_rec.at[z], s_gz.at[d], r_gz.at[d], along("z", d))

    peers(lambda d: gz_copy(d).start())
    gp_rec[z] = gp[z]

    def ga2_copy(d):
        whole = gbuf.at[x, pl.ds(0, 256)]
        return remote(whole, whole, s_ga2.at[d], r_ga2.at[d], along("x", d))

    def gb2_copy(d):
        whole = gbuf.at[:, pl.ds(256 + CHUNK * y, CHUNK)]
        return remote(whole, whole, s_gb2.at[d], r_gb2.at[d], along("y", d))

    peers(lambda d: ga1_copy(d).wait_recv())
    peers(lambda d: ga2_copy(d).start())
    peers(lambda d: gb1_copy(d).wait_recv())
    peers(lambda d: gb2_copy(d).start())

    peers(lambda d: gz_copy(d).wait_recv())
    over_z = summed(gp_rec)
    gx[:, pl.ds(0, 8), :] = over_z[:64].reshape(RING, 8, HALF)
    gx[:, pl.ds(8, 8), :] = jnp.broadcast_to(over_z[64:][None], (RING, 8, HALF))

    def gx_copy(d):
        return remote(gx.at[wrap(x + d)], gx_rec.at[x], s_gx.at[d], r_gx.at[d], along("x", d))

    peers(lambda d: gx_copy(d).start())
    gx_rec[x] = gx[x]

    adj_copy.wait_recv()

    def pull(at_x, first):
        acc[...] += jnp.dot(
            dense[at_x, :, pl.ds(first, 256)], gbuf[at_x, pl.ds(first, 256), :],
            preferred_element_type=F32,
        )

    acc[...] = jnp.zeros_like(acc)
    pull(x, 0)

    def pull_a(d):
        from_x = wrap(x - d + RING)
        ga2_copy(d).wait_recv()
        pull(from_x, 0)

    peers(pull_a)

    peers(lambda d: gx_copy(d).wait_recv())
    gy[y] = summed(gx_rec)

    def gy_copy(d):
        return remote(gy.at[y], gy.at[y], s_gy.at[d], r_gy.at[d], along("y", d))

    peers(lambda d: gy_copy(d).start())

    peers(lambda d: gb2_copy(d).wait_recv())
    peers(lambda d: pull(d, 256), 0)
    back[...] = acc[...].astype(BF).reshape(RING, 64, HALF)

    def z_copy(d):
        return remote(back.at[wrap(z + d)], rec_z.at[d], s_z.at[d], r_z.at[d], along("z", d))

    peers(lambda d: z_copy(d).start())
    rec_z[0] = back[z]

    peers(lambda d: gy_copy(d).wait_recv())
    total_y = summed(gy)
    gz[x] = total_y[:8]
    gbias[k] = total_y[8:]

    def hx_copy(d):
        return remote(gz.at[x], gz.at[x], s_hx.at[d], r_hx.at[d], along("x", d))

    peers(lambda d: hx_copy(d).start())
    bias_copy = remote(gbias.at[k], gbias.at[k], s_hs.at[1], r_hs.at[1], at(x, y, z, sib))
    bias_copy.start()

    peers(lambda d: z_copy(d).wait_recv())
    total = summed(rec_z)
    b_own[...] = total.astype(BF).reshape(2, CHUNK, HALF)
    sib_copy = remote(b_own.at[sib], b_sib, s_sib.at[0], r_sib.at[0], at(x, y, z, sib))
    sib_copy.start()

    peers(lambda d: hx_copy(d).wait_recv())
    gfull[k, z] = gz[...].reshape(64, HALF)

    def hz_copy(d):
        return remote(gfull.at[k, z], gfull.at[k, z], s_hz.at[d], r_hz.at[d], along("z", d))

    peers(lambda d: hz_copy(d).start())

    for core in (0, 1):
        @pl.when(jnp.logical_not(jnp.logical_and(is_self, k == core)))
        def _():
            remote(
                act_ret.at[core], act_ret.at[core], s_ret.at[0], r_ret.at[core], worker(core)
            ).wait_recv()
            remote(
                g_ret.at[core], g_ret.at[core], s_ret.at[2], r_ret.at[2 + core], worker(core)
            ).wait_recv()

    act_out[:, pl.ds(0, HALF)] = act_ret[0]
    act_out[:, pl.ds(HALF, HALF)] = act_ret[1]
    own_part = dot_last(g_ret[0], w_self[:, pl.ds(0, HALF)]) + dot_last(
        g_ret[1], w_self[:, pl.ds(HALF, HALF)]
    )
    sib_copy.wait_recv()
    returned = dot_last(b_own[k], w_neigh[:, lanes]) + dot_last(
        b_sib[...], w_neigh[:, pl.ds(pl.multiple_of(HALF * sib, HALF), HALF)]
    )
    gf_out[...] = (own_part + returned * norm_factor).astype(BF)

    peers(lambda d: hz_copy(d).wait_recv())
    full_copy = remote(gfull.at[k], gfull.at[k], s_hs.at[0], r_hs.at[0], at(x, y, z, sib))
    full_copy.start()
    bias_copy.wait_recv()
    for core in (0, 1):
        gb_out[:, pl.ds(HALF * core, HALF)] = gbias[core, pl.ds(0, 1), :] * grad_factor
    remote(
        gfull.at[sib], gfull.at[sib], s_hs.at[0], r_hs.at[0], at(x, y, z, sib)
    ).wait_recv()
    for core in (0, 1):
        gs_out[:, pl.ds(HALF * core, HALF)] = (
            gfull[core, pl.ds(0, 4)].reshape(F, HALF) * grad_factor
        )
        gn_out[:, pl.ds(HALF * core, HALF)] = (
            gfull[core, pl.ds(4, 4)].reshape(F, HALF) * grad_factor
        )

    def a1_done(section, carry):
        for lane in (0, 1):
            @pl.when(jnp.logical_not(jnp.logical_and(4 * k + section == x, k == lane)))
            def _():
                a1_copy(section, lane).wait_send()
        return carry

    lax.fori_loop(0, 4, a1_done, 0)

    def sends_done(d):
        for lane in (0, 1):
            b1_copy(d, lane).wait_send()
        for copy in (
            a2_copy, b2_copy, ga1_copy, gb1_copy, ga2_copy, gb2_copy, gz_copy, gx_copy, gy_copy,
            hx_copy, hz_copy, z_copy,
        ):
            copy(d).wait_send()

    peers(sends_done)
    for copy in (b1_copy_sib, adj_copy, agg_copy, sib_copy, bias_copy, full_copy):
        copy.wait_send()
    for core in (0, 1):
        @pl.when(jnp.logical_not(jnp.logical_and(is_self, k == core)))
        def _():
            for copy in t_copies(core):
                copy.wait_send()

        @pl.when(jnp.logical_not(owner_is_self(core)))
        def _():
            for copy in ret_copies(core):
                copy.wait_send()


def shards(
    features, w_self, w_neigh, bias_vector, cotangent, adj_values, src_slots, dst_slots, slot_counts
):
    block_rows = features.shape[0]
    replicas = lax.axis_size("rep")
    node_total = block_rows * lax.axis_size("row")
    slot_total = adj_values.shape[2]
    norm_factor = 1.0 / math.sqrt(slot_total * replicas / (block_rows // adj_values.shape[-1]))
    grad_factor = 1.0 / math.sqrt(node_total)

    def body(*refs):
        kernel(norm_factor, grad_factor, *refs)

    vmem = pl.BlockSpec(memory_space=pltpu.VMEM)
    smem = pl.BlockSpec(memory_space=pltpu.SMEM)
    dma = pltpu.SemaphoreType.DMA
    sems = [
        dma(()), dma((4,)), dma((4,)), dma((1,)), dma((1,)), dma((8,)), dma((8,)), dma((16,)),
        dma((16,)), dma((8,)), dma((8,)), dma((8,)), dma((8,)),
        dma((1,)), dma((1,)), dma((8,)), dma((8,)), dma((8,)), dma((8,)), dma((8,)), dma((8,)),
        dma((8,)), dma((8,)), dma((4,)), dma((4,)),
        dma((8,)), dma((8,)), dma((8,)), dma((8,)), dma((8,)), dma((8,)), dma((8,)), dma((8,)),
        dma((8,)), dma((8,)), dma((2,)), dma((2,)),
        dma((8,)), dma((8,)), dma((1,)), dma((1,)),
    ]
    scratch = [
        pltpu.VMEM((64, TILE, TILE), BF),
        pltpu.VMEM((8, NB, NB), BF),
        pltpu.VMEM((2, 4, NB, HALF), BF),
        pltpu.VMEM((8, 256, HALF), BF),
        pltpu.VMEM((8, 2, 4, CHUNK, HALF), BF),
        pltpu.VMEM((8, CHUNK, HALF), BF),
        pltpu.VMEM((8, CHUNK, HALF), BF),
        pltpu.VMEM((8, CHUNK, HALF), BF),
        pltpu.VMEM((8, CHUNK, HALF), BF),
        pltpu.VMEM((2, 64, HALF), BF),
        pltpu.VMEM((2, CHUNK, F), BF),
        pltpu.VMEM((2, CHUNK, HALF), BF),
        pltpu.VMEM((2, CHUNK, HALF), BF),
        pltpu.VMEM((2, CHUNK, HALF), BF),
        pltpu.VMEM((2, CHUNK, HALF), BF),
        pltpu.VMEM((2, CHUNK, HALF), BF),
        pltpu.VMEM((8, NB, HALF), BF),
        pltpu.VMEM((NB, HALF), F32),
        pltpu.VMEM((8, 64, HALF), BF),
        pltpu.VMEM((8, 64, HALF), BF),
        pltpu.VMEM((CHUNK, HALF), BF),
        pltpu.VMEM((2, CHUNK, HALF), BF),
        pltpu.VMEM((8, 72, HALF), F32),
        pltpu.VMEM((8, 72, HALF), F32),
        pltpu.VMEM((8, 16, HALF), F32),
        pltpu.VMEM((8, 16, HALF), F32),
        pltpu.VMEM((8, 16, HALF), F32),
        pltpu.VMEM((8, 8, HALF), F32),
        pltpu.VMEM((2, 8, 64, HALF), F32),
        pltpu.VMEM((2, 8, HALF), F32),
    ]
    outs = pl.pallas_call(
        body,
        out_shape=(
            jax.ShapeDtypeStruct((CHUNK, F), BF),
            jax.ShapeDtypeStruct((CHUNK, F), BF),
            jax.ShapeDtypeStruct((F, F), F32),
            jax.ShapeDtypeStruct((F, F), F32),
            jax.ShapeDtypeStruct((1, F), F32),
        ),
        in_specs=[vmem] * 5 + [pl.BlockSpec(memory_space=pl.ANY)] + [smem] * 3,
        out_specs=(vmem,) * 5,
        scratch_shapes=scratch + sems,
        compiler_params=pltpu.CompilerParams(
            collective_id=0, has_side_effects=True, vmem_limit_bytes=48 << 20
        ),
        cost_estimate=pl.CostEstimate(
            flops=1_500_000_000, bytes_accessed=8_000_000, transcendentals=20_000
        ),
        name="sage_layer",
    )(
        features, w_self, w_neigh, bias_vector.reshape(1, -1), cotangent, adj_values,
        src_slots, dst_slots, slot_counts,
    )
    return outs[0], outs[1], outs[2], outs[3], outs[4].reshape(-1)


def solution(mesh):
    placed = (
        P("row", None),
        P(),
        P(),
        P(),
        P("row", None),
        P("row", "rep", None, None, None),
        P("row", "rep", None),
        P("row", "rep", None),
        P("row", "rep"),
    )
    return jax.shard_map(
        shards,
        mesh=mesh,
        in_specs=placed,
        out_specs=(P(("row", "rep"), None), P(("row", "rep"), None), P(), P(), P()),
        check_vma=False,
    )
```

time: 831 us -> 104 us (0.13)
  waiting for transfers between devices: 607 us -> 0 us
  blocking collectives: 135 us -> 0 us
  Pallas kernels: 0 us -> 91.5 us
  matrix products: 37.6 us -> 0 us
  other arithmetic: 20.1 us -> 0 us
  between operations: 14.6 us -> 1.31 us
    psum x3 -> x0, waiting for transfers between devices: 491 us -> none  [the longest x2 344 us: spread(): return lax.psum(block, axis)]
    psum x1 -> x0, blocking collectives: 117 us -> none  [shards(): lax.psum((weight_terms[0], weight_terms[1], weight_terms[2]), ('row', 're...]
    reduce_scatter x2 -> x0, waiting for transfers between devices: 116 us -> none  [the longest x1 61 us: shards(): lax.psum_scatter(partial_value, 'rep', scatter_dimension=0, tiled=True)]
    pallas_call x0 -> x1, Pallas kernels: none -> 91.5 us  [shards(): pl.pallas_call(body, out_shape=(jax.ShapeDtypeStruct((CHUNK, F), BF), jax...]
    dot_general x38 -> x0, matrix products: 37.6 us -> none  [the longest x16 21 us: add_group(): jnp.einsum('gab,gbf->gaf', group_tiles, source_rows, preferred_element_ty...]
    all_gather x1 -> x0, blocking collectives: 18 us -> none  [shards(): aggregate = lax.all_gather(aggregate_part, 'rep', axis=0, tiled=True)]
    and x16 -> x0, other arithmetic: 11.7 us -> none  [add_group(): source_rows = jnp.take(buffer, group_sources, axis=0)]
    unnamed x14 -> x21, local copies, waits for them, and re-layouts: 0.04 us -> 10.5 us
  transfers between devices with their start and end apart: 5 -> 0, of which waited for: 5 -> 0; matrix products, arithmetic and copies ran while one was open for 4% -> 0% of each run, Pallas kernels for 0% -> 0%
where the time goes in v1:
time: 104 us; the launch traced here: 103 us
  Pallas kernels  91.5 us (88%)
  local copies, waits for them, and re-layouts  10.5 us (10%)
  between operations  1.31 us (1%)
    pallas_call x1, Pallas kernels, shards(): pl.pallas_call(body, out_shape=(jax.ShapeDtypeStruct((CHUNK, F), BF), jax...  91.5 us
    unnamed x21, local copies, waits for them, and re-layouts  10.5 us

profile of v1, /device:TPU:1, one launch (start us, length us, event | category | flops | bytes accessed | tf_op | source)
XLA Modules:
  0.0 103.3 jit_solution(5897365599184285509)
XLA Ops:
  1.3 0.0 copy-start
  1.3 1.6 %copy-done = bf16[1,1,64,128,128]{4,3,2,1,0:T(8,128)(2,1)S(1)} copy-done((bf16[1,1,64,128,128]{4,3,2,1,0:T(8,128)(2,1)S(1)}, bf16[1,1,64,128,128]{4,3,2,1,0:T(8,128)(2,1)}, u32[]{:S(2)}) %copy-start) | copy-done | bytes 2097176
  2.9 0.0 copy-start.1
  2.9 0.9 copy-done.1
  3.8 0.0 copy-start.2
  3.8 0.9 copy-done.2
  4.8 0.0 copy-start.3
  4.8 0.9 copy-done.3
  5.7 0.0 copy-start.4
  5.7 0.9 copy-done.4
  6.6 0.0 copy-start.5
  6.6 0.7 copy-done.5
  7.3 0.0 copy-start.6
  7.3 0.7 copy-done.6
  7.9 0.0 copy-start.7
  7.9 0.7 copy-done.7
  8.6 91.5 %sage_layer.1 = (bf16[32,256]{1,0:T(8,128)(2,1)S(1)}, bf16[32,256]{1,0:T(8,128)(2,1)S(1)}, f32[256,256]{1,0:T(8,128)S(1)}, f32[256,256]{1,0:T(8,128)S(1)}, f32[1,256]{1,0:T(1,128)S(1)}) custom-call(bf16[512,256]{1,0:T(8,128)(2,1)S(1)} %copy-done.1, bf16[256,256]{1,0:T(8,128)(2,1)S(1)} %copy-done.3, bf16[256,256]{1,0:T(8,128)(2,1)S(1)} %copy-done.4, ...), custom_call_target="tpu_custom_call" | custom-call | flops 1500000000 | bytes 8000000 | tf_op jit(solution)/shard_map/sage_layer/pallas_call | solution.py:552
  100.1 0.6 copy.20
  100.7 0.6 copy.21
  101.3 0.7 copy.22
  102.0 0.7 copy.23
  102.7 0.6 copy.24
Async XLA Ops:
  1.3 1.6 %copy-start = (bf16[1,1,64,128,128]{4,3,2,1,0:T(8,128)(2,1)S(1)}, bf16[1,1,64,128,128]{4,3,2,1,0:T(8,128)(2,1)}, u32[]{:S(2)}) copy-start(bf16[1,1,64,128,128]{4,3,2,1,0:T(8,128)(2,1)} %refs_5_.1) | copy-start | bytes 6291460
  2.9 0.9 copy-start.1
  3.8 0.9 copy-start.2
  4.8 0.9 copy-start.3
  5.7 0.9 copy-start.4
  6.6 0.7 copy-start.5
  7.3 0.7 copy-start.6
  7.9 0.7 copy-start.7

commit v2 on v1

v2 whole, which is shorter than its diff:
```python
import math

import jax
import jax.numpy as jnp
from jax import lax
from jax.experimental import pallas as pl
from jax.experimental.pallas import tpu as pltpu
from jax.sharding import PartitionSpec as P

RING = 8
HALF = 128
CHUNK = 32
TILE = 128
NB = 512
F = 256
MESH = pl.DeviceIdType.MESH
BF = jnp.bfloat16
F32 = jnp.float32


def wrap(value):
    return lax.rem(value, RING)


def dot_first(a, b):
    return lax.dot_general(a, b, (((0,), (0,)), ((), ())), preferred_element_type=F32)


def dot_last(a, b):
    return lax.dot_general(a, b, (((1,), (1,)), ((), ())), preferred_element_type=F32)


def kernel(
    norm_factor, grad_factor,
    feat_hbm, ws_hbm, wn_hbm, bias_hbm, cot_hbm, adj, src_hbm, dst_hbm, counts,
    act_out, gf_out, gs_out, gn_out, gb_out,
    feat, w_self, w_neigh, cot, bias, src_slots, dst_slots,
    tiles, dense, part, rec_a, rec_b, mid_a, mid_b, rec_a2, rec_b2, agg,
    f_rows, c_rows, g_own, a_own, act_ret, g_ret, gbuf, acc, back, rec_z, b_sib, b_own,
    gp, gp_rec, gx, gx_rec, gy, gz, gfull, gbias,
    load_sem, s_t, r_t, s_adj, r_adj, s_a1, r_a1, s_b1, r_b1, s_a2, r_a2, s_b2, r_b2,
    s_agg, r_agg, s_ga1, r_ga1, s_gb1, r_gb1, s_ga2, r_ga2, s_gb2, r_gb2, s_ret, r_ret,
    s_gz, r_gz, s_gx, r_gx, s_gy, r_gy, s_hx, r_hx, s_hz, r_hz, s_hs, r_hs,
    s_z, r_z, s_sib, r_sib,
):
    row = lax.axis_index("row")
    rep = lax.axis_index("rep")
    y, x = row // RING, lax.rem(row, RING)
    z, k = rep // 2, lax.rem(rep, 2)
    sib = 1 - k

    def at(xx, yy, zz, kk):
        return (yy * RING + xx, zz * 2 + kk)

    def along(axis, d):
        if axis == "x":
            return at(wrap(x + d), y, z, k)
        if axis == "y":
            return at(x, wrap(y + d), z, k)
        return at(x, y, wrap(z + d), k)

    def remote(src, dst, send_sem, recv_sem, device):
        return pltpu.make_async_remote_copy(
            src_ref=src, dst_ref=dst, send_sem=send_sem, recv_sem=recv_sem,
            device_id=device, device_id_type=MESH,
        )

    def peers(fn):
        def step(i, carry):
            fn(4 + (1 - 2 * lax.rem(i, 2)) * ((i + 1) // 2))
            return carry

        lax.fori_loop(0, RING - 1, step, 0)

    def unless(condition, fn):
        pl.when(jnp.logical_not(condition))(fn)

    sent = []

    class Exchange:
        def __init__(self, copy, start=None, recv=None, done=None):
            self.copy = copy
            self.start_all = start or (lambda: peers(lambda d: copy(d).start()))
            self.recv_all = recv or (lambda: peers(lambda d: copy(d).wait_recv()))
            self.done = done or (lambda: peers(lambda d: copy(d).wait_send()))
            self.pending = False

        def start(self):
            self.start_all()
            self.begun()

        def begun(self):
            self.pending = True
            sent.append(self)

        def recv(self):
            self.recv_all()
            self.pending = False

    def single(copy):
        return Exchange(None, copy.start, copy.wait_recv, copy.wait_send)

    def finish():
        for exchange in sent:
            if exchange.pending:
                exchange.recv()
        for exchange in sent:
            exchange.done()

    own_chunk = rep
    worker_y = wrap(own_chunk)
    own_half = own_chunk // RING
    is_self = jnp.logical_and(worker_y == y, y == z)

    def worker(core):
        return at(x, worker_y, y, core)

    def owner(half):
        return at(x, z, 4 * half + y // 2, lax.rem(y, 2))

    def owner_is_self(half):
        return jnp.logical_and(is_self, own_half == half)

    def worker_is_self(core):
        return jnp.logical_and(is_self, k == core)

    load_tiles = [
        pltpu.make_async_copy(
            adj.at[0, 0, pl.ds(16 * part_no, 16)], tiles.at[pl.ds(16 * part_no, 16)],
            load_sem.at[5 + part_no],
        )
        for part_no in range(4)
    ]
    load_feat = pltpu.make_async_copy(feat_hbm, feat, load_sem.at[1])
    load_cot = pltpu.make_async_copy(cot_hbm, cot, load_sem.at[2])
    load_ws = pltpu.make_async_copy(ws_hbm, w_self, load_sem.at[3])
    load_wn = pltpu.make_async_copy(wn_hbm, w_neigh, load_sem.at[4])
    load_bias = pltpu.make_async_copy(bias_hbm, bias, load_sem.at[9])
    load_src = pltpu.make_async_copy(src_hbm, src_slots, load_sem.at[10])
    load_dst = pltpu.make_async_copy(dst_hbm, dst_slots, load_sem.at[11])
    for load in (
        load_src, load_dst, load_feat, *load_tiles, load_cot, load_ws, load_wn, load_bias
    ):
        load.start()

    barrier = pltpu.get_barrier_semaphore()

    def greet(device):
        pl.semaphore_signal(barrier, inc=1, device_id=device, device_id_type=MESH)

    def greet_peers(d):
        for core in (0, 1):
            greet(at(wrap(x + d), y, z, core))
            greet(at(x, wrap(y + d), z, core))
        greet(at(x, y, wrap(z + d), k))

    peers(greet_peers)
    greet(at(x, y, z, sib))
    for core in (0, 1):
        unless(worker_is_self(core), lambda core=core: greet(worker(core)))
        unless(owner_is_self(core), lambda core=core: greet(owner(core)))

    for load in (load_src, load_dst, load_feat, *load_tiles):
        load.wait()

    live = counts[0, 0]

    def build(section, pointer):
        for t in range(4):
            for u in range(4):
                slot = jnp.minimum(pointer, 63)
                hit = jnp.logical_and(
                    pointer < live,
                    jnp.logical_and(
                        src_slots[0, 0, slot] == section * 4 + u, dst_slots[0, 0, slot] == t
                    ),
                )
                tile = tiles[slot]
                dense[4 * k + section, pl.ds(t * TILE, TILE), pl.ds(u * TILE, TILE)] = jnp.where(
                    hit, tile, jnp.zeros_like(tile)
                )
                pointer = pointer + hit.astype(jnp.int32)
        return pointer

    pointer = jnp.int32(0)
    for section in range(4):
        pointer = build(section, pointer)
        product = dot_first(dense[4 * k + section], feat[...]).astype(BF)
        part[0, section] = product[:, :HALF]
        part[1, section] = product[:, HALF:]
    for load in (load_cot, load_ws, load_wn, load_bias):
        load.wait()

    pl.semaphore_wait(barrier, 40 - 2 * is_self.astype(jnp.int32))

    mine_here = (x // 4) == k

    def a1_copy(section, lane):
        to_x = 4 * k + section
        d = wrap(to_x - x + RING)
        return remote(
            part.at[lane, section, pl.ds(0, 256)], rec_a.at[d],
            s_a1.at[section * 2 + lane], r_a1.at[d], at(to_x, y, z, lane),
        )

    def a1_each(method):
        def step(section, carry):
            for lane in (0, 1):
                unless(
                    jnp.logical_and(4 * k + section == x, k == lane),
                    lambda lane=lane: getattr(a1_copy(section, lane), method)(),
                )
            return carry

        lax.fori_loop(0, 4, step, 0)

    def a1_wait(d):
        remote(rec_a.at[d], rec_a.at[d], s_a1.at[0], r_a1.at[d], at(x, y, z, sib)).wait_recv()

    def a1_recv():
        unless(mine_here, lambda: a1_wait(0))
        peers(a1_wait)

    a1 = Exchange(
        None, lambda: a1_each("start"), a1_recv, lambda: a1_each("wait_send")
    )

    def b1_copy(d, lane):
        to_y = wrap(y + d)
        return remote(
            part.at[lane, :, pl.ds(256 + CHUNK * to_y, CHUNK)], rec_b.at[d, k],
            s_b1.at[d * 2 + lane], r_b1.at[d * 2 + k], at(x, to_y, z, lane),
        )

    def b1_start(d):
        for lane in (0, 1):
            b1_copy(d, lane).start()

    def b1_wait(d):
        for core in (0, 1):
            remote(
                rec_b.at[d, core], rec_b.at[d, core], s_b1.at[0], r_b1.at[d * 2 + core],
                at(x, y, z, sib),
            ).wait_recv()

    def b1_done(d):
        for lane in (0, 1):
            b1_copy(d, lane).wait_send()

    b1 = Exchange(
        None, lambda: peers(b1_start), lambda: peers(b1_wait), lambda: peers(b1_done)
    )
    b1_sib = Exchange(
        None,
        lambda: remote(
            part.at[sib, :, pl.ds(256 + CHUNK * y, CHUNK)], rec_b.at[0, k],
            s_b1.at[0], r_b1.at[k], at(x, y, z, sib),
        ).start(),
        lambda: remote(
            rec_b.at[0, sib], rec_b.at[0, sib], s_b1.at[0], r_b1.at[sib], at(x, y, z, sib)
        ).wait_recv(),
        lambda: remote(
            part.at[sib, :, pl.ds(256 + CHUNK * y, CHUNK)], rec_b.at[0, k],
            s_b1.at[0], r_b1.at[k], at(x, y, z, sib),
        ).wait_send(),
    )
    a1.start()
    b1.start()
    b1_sib.start()
    rec_b[0, k] = part[k, :, pl.ds(pl.multiple_of(256 + CHUNK * y, CHUNK), CHUNK), :]

    @pl.when(mine_here)
    def _():
        rec_a[0] = part[k, x - 4 * k, pl.ds(0, 256), :]

    def t_copies(core):
        rows = pl.ds(CHUNK * own_chunk, CHUNK)
        return (
            remote(feat.at[rows], f_rows.at[own_half], s_t.at[core], r_t.at[own_half], worker(core)),
            remote(
                cot.at[rows, pl.ds(HALF * core, HALF)], c_rows.at[own_half],
                s_t.at[2 + core], r_t.at[2 + own_half], worker(core),
            ),
        )

    def t_each(method):
        def step(core):
            for copy in t_copies(core):
                getattr(copy, method)()

        for core in (0, 1):
            unless(worker_is_self(core), lambda core=core: step(core))

    def t_recv():
        def step(half):
            remote(f_rows.at[half], f_rows.at[half], s_t.at[0], r_t.at[half], owner(half)).wait_recv()
            remote(
                c_rows.at[half], c_rows.at[half], s_t.at[2], r_t.at[2 + half], owner(half)
            ).wait_recv()

        for half in (0, 1):
            unless(owner_is_self(half), lambda half=half: step(half))

    fetch = Exchange(None, lambda: t_each("start"), t_recv, lambda: t_each("wait_send"))
    fetch.start()

    @pl.when(is_self)
    def _():
        rows = pl.ds(pl.multiple_of(CHUNK * own_chunk, CHUNK), CHUNK)
        f_rows[own_half] = feat[rows, :]
        c_rows[own_half] = cot[rows, pl.ds(pl.multiple_of(HALF * k, HALF), HALF)]

    adj_swap = single(
        remote(
            dense.at[pl.ds(4 * k, 4)], dense.at[pl.ds(4 * k, 4)], s_adj.at[0], r_adj.at[0],
            at(x, y, z, sib),
        )
    )
    adj_swap.start()

    fetch.recv()
    lanes = pl.ds(pl.multiple_of(HALF * k, HALF), HALF)
    rows64 = f_rows[...].reshape(64, F)
    self_part = jnp.dot(rows64, w_self[:, lanes], preferred_element_type=F32) + bias[:, lanes]

    def summed(ref):
        total = ref[0].astype(F32)
        for d in range(1, RING):
            total = total + ref[d].astype(F32)
        return total

    a1.recv()
    mid_a[...] = summed(rec_a).astype(BF).reshape(RING, CHUNK, HALF)
    a2 = Exchange(
        lambda d: remote(
            mid_a.at[wrap(y + d)], rec_a2.at[d], s_a2.at[d], r_a2.at[d], along("y", d)
        )
    )
    a2.start()
    rec_a2[0] = mid_a[y]

    b1_sib.recv()
    b1.recv()
    mid_b[...] = summed(rec_b).astype(BF).reshape(RING, CHUNK, HALF)
    b2 = Exchange(
        lambda d: remote(
            mid_b.at[wrap(x + d)], rec_b2.at[d], s_b2.at[d], r_b2.at[d], along("x", d)
        )
    )
    b2.start()
    rec_b2[0] = mid_b[x]

    a2.recv()
    agg[k, pl.ds(0, CHUNK), :] = (summed(rec_a2) * norm_factor).astype(BF)
    b2.recv()
    agg[k, pl.ds(CHUNK, CHUNK), :] = (summed(rec_b2) * norm_factor).astype(BF)
    agg_swap = single(remote(agg.at[k], agg.at[k], s_agg.at[0], r_agg.at[0], at(x, y, z, sib)))
    agg_swap.start()
    agg_swap.recv()

    pre = (
        self_part
        + jnp.dot(agg[0], w_neigh[pl.ds(0, HALF), lanes], preferred_element_type=F32)
        + jnp.dot(agg[1], w_neigh[pl.ds(HALF, HALF), lanes], preferred_element_type=F32)
    )
    low = jnp.exp(jnp.minimum(pre, 0.0))
    grad = (c_rows[...].reshape(64, HALF).astype(F32) * low).astype(BF)
    g_own[...] = grad.reshape(2, CHUNK, HALF)

    place_a = gbuf.at[x, pl.ds(CHUNK * y, CHUNK)]
    place_b = gbuf.at[x, pl.ds(256 + CHUNK * y, CHUNK)]
    ga1 = Exchange(
        lambda d: remote(g_own.at[0], place_a, s_ga1.at[d], r_ga1.at[d], along("y", d))
    )
    gb1 = Exchange(
        lambda d: remote(g_own.at[1], place_b, s_gb1.at[d], r_gb1.at[d], along("x", d))
    )
    ga1.start()
    gb1.start()
    gbuf[x, pl.ds(pl.multiple_of(CHUNK * y, CHUNK), CHUNK), :] = g_own[0]
    gbuf[x, pl.ds(pl.multiple_of(256 + CHUNK * y, CHUNK), CHUNK), :] = g_own[1]
    a_own[...] = jnp.where(pre > 0, pre, low - 1.0).astype(BF).reshape(2, CHUNK, HALF)

    def ret_copies(half):
        return (
            remote(a_own.at[half], act_ret.at[k], s_ret.at[half], r_ret.at[k], owner(half)),
            remote(g_own.at[half], g_ret.at[k], s_ret.at[2 + half], r_ret.at[2 + k], owner(half)),
        )

    def ret_each(method):
        def step(half):
            for copy in ret_copies(half):
                getattr(copy, method)()

        for half in (0, 1):
            unless(owner_is_self(half), lambda half=half: step(half))

    def ret_recv():
        def step(core):
            remote(
                act_ret.at[core], act_ret.at[core], s_ret.at[0], r_ret.at[core], worker(core)
            ).wait_recv()
            remote(
                g_ret.at[core], g_ret.at[core], s_ret.at[2], r_ret.at[2 + core], worker(core)
            ).wait_recv()

        for core in (0, 1):
            unless(worker_is_self(core), lambda core=core: step(core))

    give_back = Exchange(None, lambda: ret_each("start"), ret_recv, lambda: ret_each("wait_send"))
    give_back.start()

    @pl.when(is_self)
    def _():
        act_ret[k] = a_own[own_half]
        g_ret[k] = g_own[own_half]

    grad_s = dot_first(rows64, grad)
    grad_n = jnp.concatenate([dot_first(agg[0], grad), dot_first(agg[1], grad)], 0)
    terms = jnp.concatenate([grad_s, grad_n], 0).reshape(RING, 64, HALF)
    gp[:, pl.ds(0, 64), :] = terms
    col_sum = jnp.broadcast_to(jnp.sum(grad.astype(F32), axis=0, keepdims=True), (8, HALF))
    gp[:, pl.ds(64, 8), :] = jnp.broadcast_to(col_sum[None], (RING, 8, HALF))
    to_z = Exchange(
        lambda d: remote(gp.at[wrap(z + d)], gp_rec.at[z], s_gz.at[d], r_gz.at[d], along("z", d))
    )
    to_z.start()
    gp_rec[z] = gp[z]

    class Relay:
        def __init__(self, axis, me, piece, half, send_sem, recv_sem):
            self.axis, self.me, self.piece, self.half = axis, me, piece, half
            self.sems = (send_sem, recv_sem)
            self.pending = False
            self.done_all = []

        def copy(self, ref, sign, hop, tag):
            send_sem, recv_sem = self.sems
            index = 2 * tag + (sign < 0)
            return remote(
                ref, ref, send_sem.at[index], recv_sem.at[index],
                along(self.axis, (sign * hop) % RING),
            )

        def owner(self, sign, distance):
            return wrap(self.me + (-sign * distance) % RING)

        def near(self, sign):
            return self.copy(self.piece(self.me), sign, 1, 0)

        def next_near(self, sign):
            return self.copy(self.piece(self.me), sign, 2, 1)

        def far(self, sign):
            return self.copy(self.piece(self.owner(sign, 2)), sign, 1, 2)

        def opposite(self, sign):
            return self.copy(self.half(self.owner(sign, 2), sign), sign, 2, 3)

        def start(self):
            for sign in (1, -1):
                self.next_near(sign).start()
            for sign in (1, -1):
                self.near(sign).start()
            self.pending = True
            sent.append(self)

        def pass_on(self):
            for sign in (1, -1):
                self.next_near(sign).wait_recv()
                self.opposite(sign).start()
                self.far(sign).start()

        def recv(self):
            for sign in (1, -1):
                self.near(sign).wait_recv()
                self.far(sign).wait_recv()
                self.opposite(sign).wait_recv()
            self.pending = False

        def done(self):
            for sign in (1, -1):
                for copy in (self.near, self.next_near, self.far, self.opposite):
                    copy(sign).wait_send()

    ga2 = Relay(
        "x", x, lambda at_x: gbuf.at[at_x, pl.ds(0, 256)],
        lambda at_x, sign: gbuf.at[at_x, pl.ds(0 if sign > 0 else 128, 128)], s_ga2, r_ga2,
    )
    gb2 = Relay(
        "y", y, lambda at_y: gbuf.at[:, pl.ds(256 + CHUNK * at_y, CHUNK)],
        lambda at_y, sign: gbuf.at[
            pl.ds(0 if sign > 0 else 4, 4), pl.ds(256 + CHUNK * at_y, CHUNK)
        ], s_gb2, r_gb2,
    )
    ga1.recv()
    ga2.start()
    gb1.recv()
    gb2.start()
    ga2.pass_on()
    gb2.pass_on()

    to_z.recv()
    over_z = summed(gp_rec)
    gx[:, pl.ds(0, 8), :] = over_z[:64].reshape(RING, 8, HALF)
    gx[:, pl.ds(8, 8), :] = jnp.broadcast_to(over_z[64:][None], (RING, 8, HALF))
    to_x = Exchange(
        lambda d: remote(gx.at[wrap(x + d)], gx_rec.at[x], s_gx.at[d], r_gx.at[d], along("x", d))
    )
    to_x.start()
    gx_rec[x] = gx[x]

    adj_swap.recv()

    def pull(at_x, first):
        acc[...] += jnp.dot(
            dense[at_x, :, pl.ds(first, 256)], gbuf[at_x, pl.ds(first, 256), :],
            preferred_element_type=F32,
        )

    acc[...] = jnp.zeros_like(acc)
    pull(x, 0)

    for sign in (1, -1):
        pull(ga2.owner(sign, 2), 0)
    for sign in (1, -1):
        ga2.near(sign).wait_recv()
        pull(ga2.owner(sign, 1), 0)
    for sign in (1, -1):
        ga2.far(sign).wait_recv()
        pull(ga2.owner(sign, 3), 0)
    for sign in (1, -1):
        ga2.opposite(sign).wait_recv()
    ga2.pending = False
    pull(ga2.owner(1, 4), 0)

    to_x.recv()
    gy[y] = summed(gx_rec)
    over_y = Exchange(lambda d: remote(gy.at[y], gy.at[y], s_gy.at[d], r_gy.at[d], along("y", d)))
    over_y.start()

    gb2.recv()
    lax.fori_loop(0, RING, lambda at_x, carry: (pull(at_x, 256), carry)[1], 0)
    back[...] = acc[...].astype(BF).reshape(RING, 64, HALF)
    sums = Exchange(
        lambda d: remote(back.at[wrap(z + d)], rec_z.at[d], s_z.at[d], r_z.at[d], along("z", d))
    )
    sums.start()
    rec_z[0] = back[z]

    over_y.recv()
    total_y = summed(gy)
    gz[x] = total_y[:8]
    gbias[k] = total_y[8:]
    from_x = Exchange(lambda d: remote(gz.at[x], gz.at[x], s_hx.at[d], r_hx.at[d], along("x", d)))
    from_x.start()
    bias_swap = single(remote(gbias.at[k], gbias.at[k], s_hs.at[1], r_hs.at[1], at(x, y, z, sib)))
    bias_swap.start()

    sums.recv()
    b_own[...] = summed(rec_z).astype(BF).reshape(2, CHUNK, HALF)
    b_swap = single(remote(b_own.at[sib], b_sib, s_sib.at[0], r_sib.at[0], at(x, y, z, sib)))
    b_swap.start()

    from_x.recv()
    gfull[k, z] = gz[...].reshape(64, HALF).astype(BF)
    from_z = Exchange(
        lambda d: remote(gfull.at[k, z], gfull.at[k, z], s_hz.at[d], r_hz.at[d], along("z", d))
    )
    from_z.start()

    give_back.recv()
    act_out[:, pl.ds(0, HALF)] = act_ret[0]
    act_out[:, pl.ds(HALF, HALF)] = act_ret[1]
    own_part = dot_last(g_ret[0], w_self[:, pl.ds(0, HALF)]) + dot_last(
        g_ret[1], w_self[:, pl.ds(HALF, HALF)]
    )
    b_swap.recv()
    returned = dot_last(b_own[k], w_neigh[:, lanes]) + dot_last(
        b_sib[...], w_neigh[:, pl.ds(pl.multiple_of(HALF * sib, HALF), HALF)]
    )
    gf_out[...] = (own_part + returned * norm_factor).astype(BF)

    from_z.recv()
    full_swap = single(remote(gfull.at[k], gfull.at[k], s_hs.at[0], r_hs.at[0], at(x, y, z, sib)))
    full_swap.start()
    bias_swap.recv()
    for core in (0, 1):
        gb_out[:, pl.ds(HALF * core, HALF)] = gbias[core, pl.ds(0, 1), :] * grad_factor
    full_swap.recv()
    for core in (0, 1):
        gs_out[:, pl.ds(HALF * core, HALF)] = (
            gfull[core, pl.ds(0, 4)].reshape(F, HALF).astype(F32) * grad_factor
        )
        gn_out[:, pl.ds(HALF * core, HALF)] = (
            gfull[core, pl.ds(4, 4)].reshape(F, HALF).astype(F32) * grad_factor
        )
    finish()


def place(*refs):
    copies = [
        pltpu.make_async_copy(refs[i], refs[5 + i], refs[10].at[i]) for i in range(5)
    ]
    for copy in copies:
        copy.start()
    for copy in copies:
        copy.wait()


def shards(
    features, w_self, w_neigh, bias_vector, cotangent, adj_values, src_slots, dst_slots, slot_counts
):
    block_rows = features.shape[0]
    replicas = lax.axis_size("rep")
    node_total = block_rows * lax.axis_size("row")
    slot_total = adj_values.shape[2]
    norm_factor = 1.0 / math.sqrt(slot_total * replicas / (block_rows // adj_values.shape[-1]))
    grad_factor = 1.0 / math.sqrt(node_total)

    def body(*refs):
        kernel(norm_factor, grad_factor, *refs)

    vmem = pl.BlockSpec(memory_space=pltpu.VMEM)
    hbm = pl.BlockSpec(memory_space=pltpu.HBM)
    smem = pl.BlockSpec(memory_space=pltpu.SMEM)
    dma = pltpu.SemaphoreType.DMA
    sems = [
        dma((12,)), dma((4,)), dma((4,)), dma((1,)), dma((1,)), dma((8,)), dma((8,)), dma((16,)),
        dma((16,)), dma((8,)), dma((8,)), dma((8,)), dma((8,)),
        dma((1,)), dma((1,)), dma((8,)), dma((8,)), dma((8,)), dma((8,)), dma((8,)), dma((8,)),
        dma((8,)), dma((8,)), dma((4,)), dma((4,)),
        dma((8,)), dma((8,)), dma((8,)), dma((8,)), dma((8,)), dma((8,)), dma((8,)), dma((8,)),
        dma((8,)), dma((8,)), dma((2,)), dma((2,)),
        dma((8,)), dma((8,)), dma((1,)), dma((1,)),
    ]
    scratch = [
        pltpu.VMEM((NB, F), BF),
        pltpu.VMEM((F, F), BF),
        pltpu.VMEM((F, F), BF),
        pltpu.VMEM((NB, F), BF),
        pltpu.VMEM((1, F), F32),
        pltpu.SMEM((1, 1, 64), jnp.int32),
        pltpu.SMEM((1, 1, 64), jnp.int32),
        pltpu.VMEM((64, TILE, TILE), BF),
        pltpu.VMEM((8, NB, NB), BF),
        pltpu.VMEM((2, 4, NB, HALF), BF),
        pltpu.VMEM((8, 256, HALF), BF),
        pltpu.VMEM((8, 2, 4, CHUNK, HALF), BF),
        pltpu.VMEM((8, CHUNK, HALF), BF),
        pltpu.VMEM((8, CHUNK, HALF), BF),
        pltpu.VMEM((8, CHUNK, HALF), BF),
        pltpu.VMEM((8, CHUNK, HALF), BF),
        pltpu.VMEM((2, 64, HALF), BF),
        pltpu.VMEM((2, CHUNK, F), BF),
        pltpu.VMEM((2, CHUNK, HALF), BF),
        pltpu.VMEM((2, CHUNK, HALF), BF),
        pltpu.VMEM((2, CHUNK, HALF), BF),
        pltpu.VMEM((2, CHUNK, HALF), BF),
        pltpu.VMEM((2, CHUNK, HALF), BF),
        pltpu.VMEM((8, NB, HALF), BF),
        pltpu.VMEM((NB, HALF), F32),
        pltpu.VMEM((8, 64, HALF), BF),
        pltpu.VMEM((8, 64, HALF), BF),
        pltpu.VMEM((CHUNK, HALF), BF),
        pltpu.VMEM((2, CHUNK, HALF), BF),
        pltpu.VMEM((8, 72, HALF), F32),
        pltpu.VMEM((8, 72, HALF), F32),
        pltpu.VMEM((8, 16, HALF), F32),
        pltpu.VMEM((8, 16, HALF), F32),
        pltpu.VMEM((8, 16, HALF), F32),
        pltpu.VMEM((8, 8, HALF), F32),
        pltpu.VMEM((2, 8, 64, HALF), BF),
        pltpu.VMEM((2, 8, HALF), F32),
    ]
    outs = pl.pallas_call(
        body,
        out_shape=(
            jax.ShapeDtypeStruct((CHUNK, F), BF),
            jax.ShapeDtypeStruct((CHUNK, F), BF),
            jax.ShapeDtypeStruct((F, F), F32),
            jax.ShapeDtypeStruct((F, F), F32),
            jax.ShapeDtypeStruct((1, F), F32),
        ),
        in_specs=[hbm] * 8 + [smem],
        out_specs=(vmem,) * 5,
        scratch_shapes=scratch + sems,
        compiler_params=pltpu.CompilerParams(
            collective_id=0, has_side_effects=True, vmem_limit_bytes=48 << 20
        ),
        cost_estimate=pl.CostEstimate(
            flops=1_500_000_000, bytes_accessed=8_000_000, transcendentals=20_000
        ),
        name="sage_layer",
    )(
        *(
            pltpu.with_memory_space_constraint(array, pltpu.HBM)
            for array in (
                features, w_self, w_neigh, bias_vector.reshape(1, -1), cotangent, adj_values,
                src_slots, dst_slots,
            )
        ),
        slot_counts,
    )
    act, gf, gs, gn, gb = pl.pallas_call(
        place,
        out_shape=tuple(jax.ShapeDtypeStruct(out.shape, out.dtype) for out in outs),
        in_specs=[vmem] * 5,
        out_specs=(hbm,) * 5,
        scratch_shapes=[dma((5,))],
        compiler_params=pltpu.CompilerParams(vmem_limit_bytes=4 << 20),
        name="place_results",
    )(*outs)
    return act, gf, gs, gn, gb.reshape(-1)


def solution(mesh):
    placed = (
        P("row", None),
        P(),
        P(),
        P(),
        P("row", None),
        P("row", "rep", None, None, None),
        P("row", "rep", None),
        P("row", "rep", None),
        P("row", "rep"),
    )
    return jax.shard_map(
        shards,
        mesh=mesh,
        in_specs=placed,
        out_specs=(P(("row", "rep"), None), P(("row", "rep"), None), P(), P(), P()),
        check_vma=False,
    )
```

time: 104 us -> 87.1 us (0.84)
  local copies, waits for them, and re-layouts: 10.5 us -> 0 us
  Pallas kernels: 91.5 us -> 85.6 us
    unnamed x21 -> x0, local copies, waits for them, and re-layouts: 10.5 us -> none
    pallas_call x1, Pallas kernels: 91.5 us -> 84.8 us  [shards(): pl.pallas_call(body, out_shape=(jax.ShapeDtypeStruct((CHUNK, F), BF), jax...]
where the time goes in v2:
time: 87.1 us; the launch traced here: 86.9 us
  Pallas kernels  85.6 us (98%)
  between operations  1.29 us (1%)
    pallas_call x1, Pallas kernels, shards(): pl.pallas_call(body, out_shape=(jax.ShapeDtypeStruct((CHUNK, F), BF), jax...  84.8 us

profile of v2, /device:TPU:1, one launch (start us, length us, event | category | flops | bytes accessed | tf_op | source)
XLA Modules:
  0.0 86.9 jit_solution(15311381968641397795)
XLA Ops:
  1.3 84.8 %sage_layer.1 = (bf16[32,256]{1,0:T(8,128)(2,1)S(1)}, bf16[32,256]{1,0:T(8,128)(2,1)S(1)}, f32[256,256]{1,0:T(8,128)S(1)}, f32[256,256]{1,0:T(8,128)S(1)}, f32[1,256]{1,0:T(1,128)S(1)}) custom-call(bf16[512,256]{1,0:T(8,128)(2,1)} %refs_0_.1, bf16[256,256]{1,0:T(8,128)(2,1)} %refs_1_.1, bf16[256,256]{1,0:T(8,128)(2,1)} %refs_2_.1, f32[1,256]{1,0:T(1,128)} %bitcast.2, ...), custom_call_target="tpu_custom_call" | custom-call | flops 1500000000 | bytes 8000000 | tf_op jit(solution)/shard_map/sage_layer/pallas_call | solution.py:676
  86.1 0.8 place_results.1

commit v3 on v2

--- a/solution.py
+++ b/solution.py
@@ -36,6 +36,7 @@
     act_out, gf_out, gs_out, gn_out, gb_out,
     feat, w_self, w_neigh, cot, bias, src_slots, dst_slots,
     tiles, dense, part, rec_a, rec_b, mid_a, mid_b, rec_a2, rec_b2, agg,
+    rel_a3, rel_a4, comb_a, rel_b3, rel_b4, comb_b,
     f_rows, c_rows, g_own, a_own, act_ret, g_ret, gbuf, acc, back, rec_z, b_sib, b_own,
     gp, gp_rec, gx, gx_rec, gy, gz, gfull, gbias,
     load_sem, s_t, r_t, s_adj, r_adj, s_a1, r_a1, s_b1, r_b1, s_a2, r_a2, s_b2, r_b2,
@@ -149,12 +150,13 @@
         pl.semaphore_signal(barrier, inc=1, device_id=device, device_id_type=MESH)
 
     def greet_peers(d):
-        for core in (0, 1):
-            greet(at(wrap(x + d), y, z, core))
-            greet(at(x, wrap(y + d), z, core))
-        greet(at(x, y, wrap(z + d), k))
+        for axis in ("x", "y", "z"):
+            greet(along(axis, d))
 
     peers(greet_peers)
+    for d in (1, 2, RING - 2, RING - 1):
+        greet(at(wrap(x + d), y, z, sib))
+        greet(at(x, wrap(y + d), z, sib))
     greet(at(x, y, z, sib))
     for core in (0, 1):
         unless(worker_is_self(core), lambda core=core: greet(worker(core)))
@@ -191,82 +193,133 @@
     for load in (load_cot, load_ws, load_wn, load_bias):
         load.wait()
 
-    pl.semaphore_wait(barrier, 40 - 2 * is_self.astype(jnp.int32))
+    pl.semaphore_wait(barrier, 34 - 2 * is_self.astype(jnp.int32))
 
     mine_here = (x // 4) == k
 
-    def a1_copy(section, lane):
-        to_x = 4 * k + section
-        d = wrap(to_x - x + RING)
-        return remote(
-            part.at[lane, section, pl.ds(0, 256)], rec_a.at[d],
-            s_a1.at[section * 2 + lane], r_a1.at[d], at(to_x, y, z, lane),
-        )
-
-    def a1_each(method):
-        def step(section, carry):
-            for lane in (0, 1):
-                unless(
-                    jnp.logical_and(4 * k + section == x, k == lane),
-                    lambda lane=lane: getattr(a1_copy(section, lane), method)(),
+    class Reduce:
+        def __init__(self, axis, term, here, slot, rel3, rel4, comb, send_sem, recv_sem, width):
+            self.axis, self.term, self.here, self.slot = axis, term, here, slot
+            self.rel3, self.rel4, self.comb = rel3, rel4, comb
+            self.send_sem, self.recv_sem, self.width = send_sem, recv_sem, width
+            self.pending = False
+
+        def to(self, d, core):
+            if self.axis == "x":
+                return at(wrap(x + d), y, z, core)
+            return at(x, wrap(y + d), z, core)
+
+        def slot_sem(self, number, core):
+            return self.recv_sem.at[4 + number * self.width + (core if self.width == 2 else 0)]
+
+        def copies(self, d):
+            send, recv = self.send_sem, self.recv_sem
+            if d == 4:
+                return [
+                    remote(
+                        self.term(4).at[way], self.rel4.at[way], send.at[way], recv.at[way],
+                        self.to(6 if way else 2, k),
+                    )
+                    for way in (0, 1)
+                ]
+            if d in (3, 5):
+                way = 0 if d == 3 else 1
+                return [
+                    remote(
+                        self.term(d), self.rel3.at[way], send.at[2 + way], recv.at[2 + way],
+                        self.to(7 if way else 1, k),
+                    )
+                ]
+            if d == 0:
+                return [
+                    remote(
+                        self.term(0).at[sib], self.slot(0, k), send.at[12], self.slot_sem(0, k),
+                        self.to(0, sib),
+                    )
+                ]
+            number = {1: 1, 7: 2, 2: 3, 6: 4}[d]
+            source = self.term(d) if number < 3 else self.comb.at[number - 3]
+            return [
+                remote(
+                    source.at[lane], self.slot(number, k), send.at[2 + 2 * number + lane],
+                    self.slot_sem(number, k), self.to(d, lane),
                 )
-            return carry
-
-        lax.fori_loop(0, 4, step, 0)
-
-    def a1_wait(d):
-        remote(rec_a.at[d], rec_a.at[d], s_a1.at[0], r_a1.at[d], at(x, y, z, sib)).wait_recv()
-
-    def a1_recv():
-        unless(mine_here, lambda: a1_wait(0))
-        peers(a1_wait)
-
-    a1 = Exchange(
-        None, lambda: a1_each("start"), a1_recv, lambda: a1_each("wait_send")
-    )
-
-    def b1_copy(d, lane):
-        to_y = wrap(y + d)
-        return remote(
-            part.at[lane, :, pl.ds(256 + CHUNK * to_y, CHUNK)], rec_b.at[d, k],
-            s_b1.at[d * 2 + lane], r_b1.at[d * 2 + k], at(x, to_y, z, lane),
-        )
-
-    def b1_start(d):
-        for lane in (0, 1):
-            b1_copy(d, lane).start()
-
-    def b1_wait(d):
-        for core in (0, 1):
+                for lane in (0, 1)
+            ]
+
+        def when_here(self, d, fn):
+            condition = self.here(d)
+            if condition is None:
+                fn()
+            else:
+                pl.when(condition)(fn)
+
+        def each(self, method, *distances):
+            def step(d):
+                for copy in self.copies(d):
+                    getattr(copy, method)()
+
+            for d in distances:
+                self.when_here(d, lambda d=d: step(d))
+
+        def start(self):
+            self.each("start", 4, 3, 5, 1, 7, 0)
+            self.pending = True
+            sent.append(self)
+
+        def pass_on(self):
+            def step(way, d):
+                own, rel3, rel4 = self.term(d), self.rel3.at[way], self.rel4.at[way]
+                remote(rel4, rel4, self.send_sem.at[0], self.recv_sem.at[way], self.to(0, sib)).wait_recv()
+                remote(
+                    rel3, rel3, self.send_sem.at[0], self.recv_sem.at[2 + way], self.to(0, sib)
+                ).wait_recv()
+                for lane in (0, 1):
+                    total = own[lane].astype(F32) + rel3[lane].astype(F32)
+                    if lane == way:
+                        total = total + rel4[...].astype(F32)
+                    self.comb[way, lane] = total.astype(BF)
+                for copy in self.copies(d):
+                    copy.start()
+
+            for way, d in ((0, 2), (1, 6)):
+                self.when_here(d, lambda way=way, d=d: step(way, d))
+
+        def wait_slot(self, number, core):
+            place = self.slot(number, core)
             remote(
-                rec_b.at[d, core], rec_b.at[d, core], s_b1.at[0], r_b1.at[d * 2 + core],
-                at(x, y, z, sib),
+                place, place, self.send_sem.at[0], self.slot_sem(number, core), self.to(0, sib)
             ).wait_recv()
 
-    def b1_done(d):
-        for lane in (0, 1):
-            b1_copy(d, lane).wait_send()
-
-    b1 = Exchange(
-        None, lambda: peers(b1_start), lambda: peers(b1_wait), lambda: peers(b1_done)
-    )
-    b1_sib = Exchange(
-        None,
-        lambda: remote(
-            part.at[sib, :, pl.ds(256 + CHUNK * y, CHUNK)], rec_b.at[0, k],
-            s_b1.at[0], r_b1.at[k], at(x, y, z, sib),
-        ).start(),
-        lambda: remote(
-            rec_b.at[0, sib], rec_b.at[0, sib], s_b1.at[0], r_b1.at[sib], at(x, y, z, sib)
-        ).wait_recv(),
-        lambda: remote(
-            part.at[sib, :, pl.ds(256 + CHUNK * y, CHUNK)], rec_b.at[0, k],
-            s_b1.at[0], r_b1.at[k], at(x, y, z, sib),
-        ).wait_send(),
+        def recv(self):
+            if self.width == 2:
+                self.wait_slot(0, sib)
+            else:
+                unless(mine_here, lambda: self.wait_slot(0, 0))
+            for number in (1, 2, 3, 4):
+                for core in range(self.width):
+                    self.wait_slot(number, core)
+            self.pending = False
+
+        def done(self):
+            self.each("wait_send", *range(RING))
+
+    def term_a(d):
+        return part.at[:, lax.rem(x + d, 4), pl.ds(0, 256)]
+
+    def term_b(d):
+        return part.at[:, :, pl.ds(pl.multiple_of(256 + CHUNK * wrap(y + d), CHUNK), CHUNK)]
+
+    a1 = Reduce(
+        "x", term_a, lambda d: (wrap(x + d) // 4) == k, lambda number, core: rec_a.at[number],
+        rel_a3, rel_a4, comb_a, s_a1, r_a1, 1,
+    )
+    b1 = Reduce(
+        "y", term_b, lambda d: None, lambda number, core: rec_b.at[number, core],
+        rel_b3, rel_b4, comb_b, s_b1, r_b1, 2,
     )
     a1.start()
     b1.start()
-    b1_sib.start()
     rec_b[0, k] = part[k, :, pl.ds(pl.multiple_of(256 + CHUNK * y, CHUNK), CHUNK), :]
 
     @pl.when(mine_here)
@@ -317,6 +370,8 @@
         )
     )
     adj_swap.start()
+    a1.pass_on()
+    b1.pass_on()
 
     fetch.recv()
     lanes = pl.ds(pl.multiple_of(HALF * k, HALF), HALF)
@@ -325,7 +380,7 @@
 
     def summed(ref):
         total = ref[0].astype(F32)
-        for d in range(1, RING):
+        for d in range(1, ref.shape[0]):
             total = total + ref[d].astype(F32)
         return total
 
@@ -339,7 +394,6 @@
     a2.start()
     rec_a2[0] = mid_a[y]
 
-    b1_sib.recv()
     b1.recv()
     mid_b[...] = summed(rec_b).astype(BF).reshape(RING, CHUNK, HALF)
     b2 = Exchange(
@@ -626,8 +680,8 @@
     smem = pl.BlockSpec(memory_space=pltpu.SMEM)
     dma = pltpu.SemaphoreType.DMA
     sems = [
-        dma((12,)), dma((4,)), dma((4,)), dma((1,)), dma((1,)), dma((8,)), dma((8,)), dma((16,)),
-        dma((16,)), dma((8,)), dma((8,)), dma((8,)), dma((8,)),
+        dma((12,)), dma((4,)), dma((4,)), dma((1,)), dma((1,)), dma((13,)), dma((9,)), dma((13,)),
+        dma((14,)), dma((8,)), dma((8,)), dma((8,)), dma((8,)),
         dma((1,)), dma((1,)), dma((8,)), dma((8,)), dma((8,)), dma((8,)), dma((8,)), dma((8,)),
         dma((8,)), dma((8,)), dma((4,)), dma((4,)),
         dma((8,)), dma((8,)), dma((8,)), dma((8,)), dma((8,)), dma((8,)), dma((8,)), dma((8,)),
@@ -645,13 +699,19 @@
         pltpu.VMEM((64, TILE, TILE), BF),
         pltpu.VMEM((8, NB, NB), BF),
         pltpu.VMEM((2, 4, NB, HALF), BF),
-        pltpu.VMEM((8, 256, HALF), BF),
-        pltpu.VMEM((8, 2, 4, CHUNK, HALF), BF),
+        pltpu.VMEM((5, 256, HALF), BF),
+        pltpu.VMEM((5, 2, 4, CHUNK, HALF), BF),
         pltpu.VMEM((8, CHUNK, HALF), BF),
         pltpu.VMEM((8, CHUNK, HALF), BF),
         pltpu.VMEM((8, CHUNK, HALF), BF),
         pltpu.VMEM((8, CHUNK, HALF), BF),
         pltpu.VMEM((2, 64, HALF), BF),
+        pltpu.VMEM((2, 2, 256, HALF), BF),
+        pltpu.VMEM((2, 256, HALF), BF),
+        pltpu.VMEM((2, 2, 256, HALF), BF),
+        pltpu.VMEM((2, 2, 4, CHUNK, HALF), BF),
+        pltpu.VMEM((2, 4, CHUNK, HALF), BF),
+        pltpu.VMEM((2, 2, 4, CHUNK, HALF), BF),
         pltpu.VMEM((2, CHUNK, F), BF),
         pltpu.VMEM((2, CHUNK, HALF), BF),
         pltpu.VMEM((2, CHUNK, HALF), BF),

time: 87.1 us -> 81.8 us (0.939)
  Pallas kernels: 85.6 us -> 80.4 us
    pallas_call x1, Pallas kernels: 84.8 us -> 79.5 us  [shards(): pl.pallas_call(body, out_shape=(jax.ShapeDtypeStruct((CHUNK, F), BF), jax...]
where the time goes in v3:
time: 81.8 us; the launch traced here: 81.6 us
  Pallas kernels  80.4 us (98%)
  between operations  1.29 us (2%)
    pallas_call x1, Pallas kernels, shards(): pl.pallas_call(body, out_shape=(jax.ShapeDtypeStruct((CHUNK, F), BF), jax...  79.5 us

profile of v3, /device:TPU:1, one launch (start us, length us, event | category | flops | bytes accessed | tf_op | source)
XLA Modules:
  0.0 81.6 jit_solution(17877609611126782000)
XLA Ops:
  1.3 79.5 %sage_layer.1 = (bf16[32,256]{1,0:T(8,128)(2,1)S(1)}, bf16[32,256]{1,0:T(8,128)(2,1)S(1)}, f32[256,256]{1,0:T(8,128)S(1)}, f32[256,256]{1,0:T(8,128)S(1)}, f32[1,256]{1,0:T(1,128)S(1)}) custom-call(bf16[512,256]{1,0:T(8,128)(2,1)} %refs_0_.1, bf16[256,256]{1,0:T(8,128)(2,1)} %refs_1_.1, bf16[256,256]{1,0:T(8,128)(2,1)} %refs_2_.1, f32[1,256]{1,0:T(1,128)} %bitcast.2, ...), custom_call_target="tpu_custom_call" | custom-call | flops 1500000000 | bytes 8000000 | tf_op jit(solution)/shard_map/sage_layer/pallas_call | solution.py:736
  80.8 0.8 %place_results.1 = (bf16[32,256]{1,0:T(8,128)(2,1)}, bf16[32,256]{1,0:T(8,128)(2,1)}, f32[256,256]{1,0:T(8,128)}, f32[256,256]{1,0:T(8,128)}, f32[1,256]{1,0:T(1,128)}) custom-call(bf16[32,256]{1,0:T(8,128)(2,1)S(1)} %get-tuple-element.15.refs_0_, bf16[32,256]{1,0:T(8,128)(2,1)S(1)} %get-tuple-element.16.refs_1_, f32[256,256]{1,0:T(8,128)S(1)} %get-tuple-element.17.refs_2_, ...), custom_call_target="tpu_custom_call" | custom-call | tf_op jit(solution)/shard_map/place_results/pallas_call | solution.py:765

commit v4 on v3

--- a/solution.py
+++ b/solution.py
@@ -38,11 +38,11 @@
     tiles, dense, part, rec_a, rec_b, mid_a, mid_b, rec_a2, rec_b2, agg,
     rel_a3, rel_a4, comb_a, rel_b3, rel_b4, comb_b,
     f_rows, c_rows, g_own, a_own, act_ret, g_ret, gbuf, acc, back, rec_z, b_sib, b_own,
-    gp, gp_rec, gx, gx_rec, gy, gz, gfull, gbias,
+    gp, gp_rec, hx1, hy1, hy2, hx2, gfull, gbias,
     load_sem, s_t, r_t, s_adj, r_adj, s_a1, r_a1, s_b1, r_b1, s_a2, r_a2, s_b2, r_b2,
     s_agg, r_agg, s_ga1, r_ga1, s_gb1, r_gb1, s_ga2, r_ga2, s_gb2, r_gb2, s_ret, r_ret,
     s_gz, r_gz, s_gx, r_gx, s_gy, r_gy, s_hx, r_hx, s_hz, r_hz, s_hs, r_hs,
-    s_z, r_z, s_sib, r_sib,
+    s_z, r_z, s_sib, r_sib, s_hy, r_hy,
 ):
     row = lax.axis_index("row")
     rep = lax.axis_index("rep")
@@ -184,12 +184,16 @@
                 pointer = pointer + hit.astype(jnp.int32)
         return pointer
 
+    def push(section, first):
+        rows = pl.ds(first, 256)
+        product = dot_first(dense[4 * k + section, :, rows], feat[...]).astype(BF)
+        part[0, section, rows] = product[:, :HALF]
+        part[1, section, rows] = product[:, HALF:]
+
     pointer = jnp.int32(0)
     for section in range(4):
         pointer = build(section, pointer)
-        product = dot_first(dense[4 * k + section], feat[...]).astype(BF)
-        part[0, section] = product[:, :HALF]
-        part[1, section] = product[:, HALF:]
+        push(section, 256)
     for load in (load_cot, load_ws, load_wn, load_bias):
         load.wait()
 
@@ -318,8 +322,10 @@
         "y", term_b, lambda d: None, lambda number, core: rec_b.at[number, core],
         rel_b3, rel_b4, comb_b, s_b1, r_b1, 2,
     )
+    b1.start()
+    for section in range(4):
+        push(section, 0)
     a1.start()
-    b1.start()
     rec_b[0, k] = part[k, :, pl.ds(pl.multiple_of(256 + CHUNK * y, CHUNK), CHUNK), :]
 
     @pl.when(mine_here)
@@ -472,9 +478,9 @@
     grad_s = dot_first(rows64, grad)
     grad_n = jnp.concatenate([dot_first(agg[0], grad), dot_first(agg[1], grad)], 0)
     terms = jnp.concatenate([grad_s, grad_n], 0).reshape(RING, 64, HALF)
-    gp[:, pl.ds(0, 64), :] = terms
-    col_sum = jnp.broadcast_to(jnp.sum(grad.astype(F32), axis=0, keepdims=True), (8, HALF))
-    gp[:, pl.ds(64, 8), :] = jnp.broadcast_to(col_sum[None], (RING, 8, HALF))
+    gp[:, pl.ds(0, 64), :] = terms.astype(BF)
+    col_sum = jnp.broadcast_to(jnp.sum(grad.astype(F32), axis=0, keepdims=True), (16, HALF))
+    gp[:, pl.ds(64, 16), :] = jnp.broadcast_to(col_sum[None], (RING, 16, HALF)).astype(BF)
     to_z = Exchange(
         lambda d: remote(gp.at[wrap(z + d)], gp_rec.at[z], s_gz.at[d], r_gz.at[d], along("z", d))
     )
@@ -551,18 +557,18 @@
     ga2.start()
     gb1.recv()
     gb2.start()
+
+    to_z.recv()
+    over_z = summed(gp_rec).astype(BF)
+    hx1[x, pl.ds(0, 32), :] = over_z[:32]
+    hx1[x, pl.ds(32, 16), :] = over_z[64:]
+    hy2[y] = over_z[32:64]
+    over_x1 = Exchange(lambda d: remote(hx1.at[x], hx1.at[x], s_gx.at[d], r_gx.at[d], along("x", d)))
+    over_y2 = Exchange(lambda d: remote(hy2.at[y], hy2.at[y], s_hy.at[d], r_hy.at[d], along("y", d)))
+    over_x1.start()
+    over_y2.start()
     ga2.pass_on()
     gb2.pass_on()
-
-    to_z.recv()
-    over_z = summed(gp_rec)
-    gx[:, pl.ds(0, 8), :] = over_z[:64].reshape(RING, 8, HALF)
-    gx[:, pl.ds(8, 8), :] = jnp.broadcast_to(over_z[64:][None], (RING, 8, HALF))
-    to_x = Exchange(
-        lambda d: remote(gx.at[wrap(x + d)], gx_rec.at[x], s_gx.at[d], r_gx.at[d], along("x", d))
-    )
-    to_x.start()
-    gx_rec[x] = gx[x]
 
     adj_swap.recv()
 
@@ -580,6 +586,16 @@
     for sign in (1, -1):
         ga2.near(sign).wait_recv()
         pull(ga2.owner(sign, 1), 0)
+
+    over_x1.recv()
+    hy1[y] = summed(hx1).astype(BF)
+    over_y1 = Exchange(lambda d: remote(hy1.at[y], hy1.at[y], s_gy.at[d], r_gy.at[d], along("y", d)))
+    over_y1.start()
+    over_y2.recv()
+    hx2[x] = summed(hy2).astype(BF)
+    over_x2 = Exchange(lambda d: remote(hx2.at[x], hx2.at[x], s_hx.at[d], r_hx.at[d], along("x", d)))
+    over_x2.start()
+
     for sign in (1, -1):
         ga2.far(sign).wait_recv()
         pull(ga2.owner(sign, 3), 0)
@@ -588,11 +604,6 @@
     ga2.pending = False
     pull(ga2.owner(1, 4), 0)
 
-    to_x.recv()
-    gy[y] = summed(gx_rec)
-    over_y = Exchange(lambda d: remote(gy.at[y], gy.at[y], s_gy.at[d], r_gy.at[d], along("y", d)))
-    over_y.start()
-
     gb2.recv()
     lax.fori_loop(0, RING, lambda at_x, carry: (pull(at_x, 256), carry)[1], 0)
     back[...] = acc[...].astype(BF).reshape(RING, 64, HALF)
@@ -602,12 +613,17 @@
     sums.start()
     rec_z[0] = back[z]
 
-    over_y.recv()
-    total_y = summed(gy)
-    gz[x] = total_y[:8]
-    gbias[k] = total_y[8:]
-    from_x = Exchange(lambda d: remote(gz.at[x], gz.at[x], s_hx.at[d], r_hx.at[d], along("x", d)))
-    from_x.start()
+    over_y1.recv()
+    total_1 = summed(hy1)
+    over_x2.recv()
+    total_2 = summed(hx2)
+    gfull[k, z, pl.ds(0, 32), :] = total_1[:32].astype(BF)
+    gfull[k, z, pl.ds(32, 32), :] = total_2.astype(BF)
+    gbias[k] = total_1[32:40]
+    from_z = Exchange(
+        lambda d: remote(gfull.at[k, z], gfull.at[k, z], s_hz.at[d], r_hz.at[d], along("z", d))
+    )
+    from_z.start()
     bias_swap = single(remote(gbias.at[k], gbias.at[k], s_hs.at[1], r_hs.at[1], at(x, y, z, sib)))
     bias_swap.start()
 
@@ -616,12 +632,6 @@
     b_swap = single(remote(b_own.at[sib], b_sib, s_sib.at[0], r_sib.at[0], at(x, y, z, sib)))
     b_swap.start()
 
-    from_x.recv()
-    gfull[k, z] = gz[...].reshape(64, HALF).astype(BF)
-    from_z = Exchange(
-        lambda d: remote(gfull.at[k, z], gfull.at[k, z], s_hz.at[d], r_hz.at[d], along("z", d))
-    )
-    from_z.start()
 
     give_back.recv()
     act_out[:, pl.ds(0, HALF)] = act_ret[0]
@@ -686,7 +696,7 @@
         dma((8,)), dma((8,)), dma((4,)), dma((4,)),
         dma((8,)), dma((8,)), dma((8,)), dma((8,)), dma((8,)), dma((8,)), dma((8,)), dma((8,)),
         dma((8,)), dma((8,)), dma((2,)), dma((2,)),
-        dma((8,)), dma((8,)), dma((1,)), dma((1,)),
+        dma((8,)), dma((8,)), dma((1,)), dma((1,)), dma((8,)), dma((8,)),
     ]
     scratch = [
         pltpu.VMEM((NB, F), BF),
@@ -724,12 +734,12 @@
         pltpu.VMEM((8, 64, HALF), BF),
         pltpu.VMEM((CHUNK, HALF), BF),
         pltpu.VMEM((2, CHUNK, HALF), BF),
-        pltpu.VMEM((8, 72, HALF), F32),
-        pltpu.VMEM((8, 72, HALF), F32),
-        pltpu.VMEM((8, 16, HALF), F32),
-        pltpu.VMEM((8, 16, HALF), F32),
-        pltpu.VMEM((8, 16, HALF), F32),
-        pltpu.VMEM((8, 8, HALF), F32),
+        pltpu.VMEM((8, 80, HALF), BF),
+        pltpu.VMEM((8, 80, HALF), BF),
+        pltpu.VMEM((8, 48, HALF), BF),
+        pltpu.VMEM((8, 48, HALF), BF),
+        pltpu.VMEM((8, 32, HALF), BF),
+        pltpu.VMEM((8, 32, HALF), BF),
         pltpu.VMEM((2, 8, 64, HALF), BF),
         pltpu.VMEM((2, 8, HALF), F32),
     ]

time: 81.8 us -> 76.7 us (0.938)
  Pallas kernels: 80.4 us -> 75.2 us
    pallas_call x1, Pallas kernels: 79.5 us -> 74.3 us  [shards(): pl.pallas_call(body, out_shape=(jax.ShapeDtypeStruct((CHUNK, F), BF), jax...]
where the time goes in v4:
time: 76.7 us; the launch traced here: 76.5 us
  Pallas kernels  75.2 us (98%)
  between operations  1.29 us (2%)
    pallas_call x1, Pallas kernels, shards(): pl.pallas_call(body, out_shape=(jax.ShapeDtypeStruct((CHUNK, F), BF), jax...  74.3 us

profile of v4, /device:TPU:1, one launch (start us, length us, event | category | flops | bytes accessed | tf_op | source)
XLA Modules:
  0.0 76.5 jit_solution(17784822532263154172)
XLA Ops:
  1.3 74.3 %sage_layer.1 = (bf16[32,256]{1,0:T(8,128)(2,1)S(1)}, bf16[32,256]{1,0:T(8,128)(2,1)S(1)}, f32[256,256]{1,0:T(8,128)S(1)}, f32[256,256]{1,0:T(8,128)S(1)}, f32[1,256]{1,0:T(1,128)S(1)}) custom-call(bf16[512,256]{1,0:T(8,128)(2,1)} %refs_0_.1, bf16[256,256]{1,0:T(8,128)(2,1)} %refs_1_.1, bf16[256,256]{1,0:T(8,128)(2,1)} %refs_2_.1, f32[1,256]{1,0:T(1,128)} %bitcast.2, ...), custom_call_target="tpu_custom_call" | custom-call | flops 1500000000 | bytes 8000000 | tf_op jit(solution)/shard_map/sage_layer/pallas_call | solution.py:746
  75.6 0.8 %place_results.1 = (bf16[32,256]{1,0:T(8,128)(2,1)}, bf16[32,256]{1,0:T(8,128)(2,1)}, f32[256,256]{1,0:T(8,128)}, f32[256,256]{1,0:T(8,128)}, f32[1,256]{1,0:T(1,128)}) custom-call(bf16[32,256]{1,0:T(8,128)(2,1)S(1)} %get-tuple-element.15.refs_0_, bf16[32,256]{1,0:T(8,128)(2,1)S(1)} %get-tuple-element.16.refs_1_, f32[256,256]{1,0:T(8,128)S(1)} %get-tuple-element.17.refs_2_, ...), custom_call_target="tpu_custom_call" | custom-call | tf_op jit(solution)/shard_map/place_results/pallas_call | solution.py:775

commit v5 on v4

--- a/solution.py
+++ b/solution.py
@@ -77,6 +77,7 @@
         pl.when(jnp.logical_not(condition))(fn)
 
     sent = []
+    settled = []
 
     class Exchange:
         def __init__(self, copy, start=None, recv=None, done=None):
@@ -101,12 +102,17 @@
     def single(copy):
         return Exchange(None, copy.start, copy.wait_recv, copy.wait_send)
 
+    def settle():
+        for exchange in sent:
+            if not exchange.pending and exchange not in settled:
+                settled.append(exchange)
+                exchange.done()
+
     def finish():
         for exchange in sent:
             if exchange.pending:
                 exchange.recv()
-        for exchange in sent:
-            exchange.done()
+        settle()
 
     own_chunk = rep
     worker_y = wrap(own_chunk)
@@ -178,7 +184,7 @@
                     ),
                 )
                 tile = tiles[slot]
-                dense[4 * k + section, pl.ds(t * TILE, TILE), pl.ds(u * TILE, TILE)] = jnp.where(
+                dense[section, pl.ds(t * TILE, TILE), pl.ds(u * TILE, TILE)] = jnp.where(
                     hit, tile, jnp.zeros_like(tile)
                 )
                 pointer = pointer + hit.astype(jnp.int32)
@@ -186,7 +192,7 @@
 
     def push(section, first):
         rows = pl.ds(first, 256)
-        product = dot_first(dense[4 * k + section, :, rows], feat[...]).astype(BF)
+        product = dot_first(dense[section, :, rows], feat[...]).astype(BF)
         part[0, section, rows] = product[:, :HALF]
         part[1, section, rows] = product[:, HALF:]
 
@@ -371,18 +377,13 @@
 
     adj_swap = single(
         remote(
-            dense.at[pl.ds(4 * k, 4)], dense.at[pl.ds(4 * k, 4)], s_adj.at[0], r_adj.at[0],
+            dense.at[pl.ds(0, 4)], dense.at[pl.ds(4, 4)], s_adj.at[0], r_adj.at[0],
             at(x, y, z, sib),
         )
     )
+    b1.pass_on()
+    a1.pass_on()
     adj_swap.start()
-    a1.pass_on()
-    b1.pass_on()
-
-    fetch.recv()
-    lanes = pl.ds(pl.multiple_of(HALF * k, HALF), HALF)
-    rows64 = f_rows[...].reshape(64, F)
-    self_part = jnp.dot(rows64, w_self[:, lanes], preferred_element_type=F32) + bias[:, lanes]
 
     def summed(ref):
         total = ref[0].astype(F32)
@@ -390,6 +391,15 @@
             total = total + ref[d].astype(F32)
         return total
 
+    b1.recv()
+    mid_b[...] = summed(rec_b).astype(BF).reshape(RING, CHUNK, HALF)
+    b2 = Exchange(
+        lambda d: remote(
+            mid_b.at[wrap(x + d)], rec_b2.at[d], s_b2.at[d], r_b2.at[d], along("x", d)
+        )
+    )
+    b2.start()
+    rec_b2[0] = mid_b[x]
     a1.recv()
     mid_a[...] = summed(rec_a).astype(BF).reshape(RING, CHUNK, HALF)
     a2 = Exchange(
@@ -400,15 +410,10 @@
     a2.start()
     rec_a2[0] = mid_a[y]
 
-    b1.recv()
-    mid_b[...] = summed(rec_b).astype(BF).reshape(RING, CHUNK, HALF)
-    b2 = Exchange(
-        lambda d: remote(
-            mid_b.at[wrap(x + d)], rec_b2.at[d], s_b2.at[d], r_b2.at[d], along("x", d)
-        )
-    )
-    b2.start()
-    rec_b2[0] = mid_b[x]
+    fetch.recv()
+    lanes = pl.ds(pl.multiple_of(HALF * k, HALF), HALF)
+    rows64 = f_rows[...].reshape(64, F)
+    self_part = jnp.dot(rows64, w_self[:, lanes], preferred_element_type=F32) + bias[:, lanes]
 
     a2.recv()
     agg[k, pl.ds(0, CHUNK), :] = (summed(rec_a2) * norm_factor).astype(BF)
@@ -439,6 +444,18 @@
     gb1.start()
     gbuf[x, pl.ds(pl.multiple_of(CHUNK * y, CHUNK), CHUNK), :] = g_own[0]
     gbuf[x, pl.ds(pl.multiple_of(256 + CHUNK * y, CHUNK), CHUNK), :] = g_own[1]
+    grad_s = dot_first(rows64, grad)
+    grad_n = jnp.concatenate([dot_first(agg[0], grad), dot_first(agg[1], grad)], 0)
+    terms = jnp.concatenate([grad_s, grad_n], 0).reshape(RING, 64, HALF)
+    gp[:, pl.ds(0, 64), :] = terms.astype(BF)
+    col_sum = jnp.broadcast_to(jnp.sum(grad.astype(F32), axis=0, keepdims=True), (16, HALF))
+    gp[:, pl.ds(64, 16), :] = jnp.broadcast_to(col_sum[None], (RING, 16, HALF)).astype(BF)
+    to_z = Exchange(
+        lambda d: remote(gp.at[wrap(z + d)], gp_rec.at[z], s_gz.at[d], r_gz.at[d], along("z", d))
+    )
+    to_z.start()
+    gp_rec[z] = gp[z]
+
     a_own[...] = jnp.where(pre > 0, pre, low - 1.0).astype(BF).reshape(2, CHUNK, HALF)
 
     def ret_copies(half):
@@ -475,17 +492,6 @@
         act_ret[k] = a_own[own_half]
         g_ret[k] = g_own[own_half]
 
-    grad_s = dot_first(rows64, grad)
-    grad_n = jnp.concatenate([dot_first(agg[0], grad), dot_first(agg[1], grad)], 0)
-    terms = jnp.concatenate([grad_s, grad_n], 0).reshape(RING, 64, HALF)
-    gp[:, pl.ds(0, 64), :] = terms.astype(BF)
-    col_sum = jnp.broadcast_to(jnp.sum(grad.astype(F32), axis=0, keepdims=True), (16, HALF))
-    gp[:, pl.ds(64, 16), :] = jnp.broadcast_to(col_sum[None], (RING, 16, HALF)).astype(BF)
-    to_z = Exchange(
-        lambda d: remote(gp.at[wrap(z + d)], gp_rec.at[z], s_gz.at[d], r_gz.at[d], along("z", d))
-    )
-    to_z.start()
-    gp_rec[z] = gp[z]
 
     class Relay:
         def __init__(self, axis, me, piece, half, send_sem, recv_sem):
@@ -553,6 +559,7 @@
             pl.ds(0 if sign > 0 else 4, 4), pl.ds(256 + CHUNK * at_y, CHUNK)
         ], s_gb2, r_gb2,
     )
+    settle()
     ga1.recv()
     ga2.start()
     gb1.recv()
@@ -572,9 +579,12 @@
 
     adj_swap.recv()
 
+    def strip(at_x):
+        return lax.rem(at_x, 4) + 4 * lax.rem(at_x // 4 + k, 2)
+
     def pull(at_x, first):
         acc[...] += jnp.dot(
-            dense[at_x, :, pl.ds(first, 256)], gbuf[at_x, pl.ds(first, 256), :],
+            dense[strip(at_x), :, pl.ds(first, 256)], gbuf[at_x, pl.ds(first, 256), :],
             preferred_element_type=F32,
         )
 
@@ -613,6 +623,7 @@
     sums.start()
     rec_z[0] = back[z]
 
+    settle()
     over_y1.recv()
     total_1 = summed(hy1)
     over_x2.recv()
@@ -645,6 +656,7 @@
     )
     gf_out[...] = (own_part + returned * norm_factor).astype(BF)
 
+    settle()
     from_z.recv()
     full_swap = single(remote(gfull.at[k], gfull.at[k], s_hs.at[0], r_hs.at[0], at(x, y, z, sib)))
     full_swap.start()

time: 76.7 us -> 74.9 us (0.977)
  Pallas kernels: 75.2 us -> 73.4 us
    pallas_call x1, Pallas kernels: 74.3 us -> 72.5 us  [shards(): pl.pallas_call(body, out_shape=(jax.ShapeDtypeStruct((CHUNK, F), BF), jax...]
where the time goes in v5:
time: 74.9 us; the launch traced here: 74.7 us
  Pallas kernels  73.4 us (98%)
  between operations  1.29 us (2%)
    pallas_call x1, Pallas kernels, shards(): pl.pallas_call(body, out_shape=(jax.ShapeDtypeStruct((CHUNK, F), BF), jax...  72.5 us

profile of v5, /device:TPU:1, one launch (start us, length us, event | category | flops | bytes accessed | tf_op | source)
XLA Modules:
  0.0 74.7 jit_solution(3205967098679899065)
XLA Ops:
  1.3 72.5 %sage_layer.1 = (bf16[32,256]{1,0:T(8,128)(2,1)S(1)}, bf16[32,256]{1,0:T(8,128)(2,1)S(1)}, f32[256,256]{1,0:T(8,128)S(1)}, f32[256,256]{1,0:T(8,128)S(1)}, f32[1,256]{1,0:T(1,128)S(1)}) custom-call(bf16[512,256]{1,0:T(8,128)(2,1)} %refs_0_.1, bf16[256,256]{1,0:T(8,128)(2,1)} %refs_1_.1, bf16[256,256]{1,0:T(8,128)(2,1)} %refs_2_.1, f32[1,256]{1,0:T(1,128)} %bitcast.2, ...), custom_call_target="tpu_custom_call" | custom-call | flops 1500000000 | bytes 8000000 | tf_op jit(solution)/shard_map/sage_layer/pallas_call | solution.py:758
  73.8 0.8 %place_results.1 = (bf16[32,256]{1,0:T(8,128)(2,1)}, bf16[32,256]{1,0:T(8,128)(2,1)}, f32[256,256]{1,0:T(8,128)}, f32[256,256]{1,0:T(8,128)}, f32[1,256]{1,0:T(1,128)}) custom-call(bf16[32,256]{1,0:T(8,128)(2,1)S(1)} %get-tuple-element.15.refs_0_, bf16[32,256]{1,0:T(8,128)(2,1)S(1)} %get-tuple-element.16.refs_1_, f32[256,256]{1,0:T(8,128)S(1)} %get-tuple-element.17.refs_2_, ...), custom_call_target="tpu_custom_call" | custom-call | tf_op jit(solution)/shard_map/place_results/pallas_call | solution.py:787
